TPU v7x, 512 devices: a whole 4x4x16 slice. The times are simulated.
512 devices in a mesh: pipe: 16 (over z_lo, y), ctx: 16 (over x, z_hi), tp: 2 (over core).
Axes of the slice: x: 4, y: 4, z: 16 (z_hi: 4, z_lo: 4; z = z_hi * 4 + z_lo), core: 2. Of those that a mesh axis runs over, the one named last changes fastest.
Arguments:
- pending_activity: bfloat16 [16, 1, 1024, 8192], P('pipe', None, 'ctx', 'tp'), may hold values from -6 to 6
- entry_rescale_vector: bfloat16 [16, 1, 8192], P('pipe', None, 'tp'), may hold values from 0.099609375 to 1.8984375
- probe_lifting_matrices: bfloat16 [16, 1, 64, 128, 64], P('pipe', None, 'tp')
- lookup_lifting_matrices: bfloat16 [16, 1, 64, 128, 64], P('pipe', None, 'tp')
- usable_extents: int32 [16, 1], P('pipe'), may hold values from 256 to 1024, as said below
- payoff_readout_vector: bfloat16 [8192], P('tp'), may hold values from -0.0625 to 0.0625
Outputs:
- handed: bfloat16 [16, 1, 1024, 8192], P('pipe', None, 'ctx', 'tp')
- scores: float32 [16, 1], P('pipe')
Inputs may be any that keep to these rules, and one draw needn't show every extreme that they name: `usable_extents`: in some section every trace is valid at all 1024 positions.
All inputs are finite; a program needn't handle non-finite values.
Results may differ from a plain program's by a relative error of at most 0.007.
Values may be sent and summed in bfloat16 or wider, within the bound.
No kernel may reach another device: no remote copies, remote signals or barrier semaphores. Data moves between devices by JAX's collectives and lax.ppermute only.
A program may use at most 128 MiB of HBM per device.

v0:
```python
import jax
import jax.numpy as jnp
from jax import lax
from jax.sharding import PartitionSpec as P

EMBED_DIMENSION = 8192
HEAD = 128


eps_norm = 1e-05


def carried_in(value, axis, join, neutral):
    count, mine = (lax.axis_size(axis), lax.axis_index(axis))
    pieces = jax.tree.map(lambda part: lax.all_gather(part, axis), value)
    running = jax.tree.map(
        lambda part, zero: jnp.full_like(part, 0) + jnp.asarray(zero, part.dtype), value, neutral
    )

    def step(position, running):
        longer = join(running, jax.tree.map(lambda part: part[position], pieces))
        return jax.tree.map(lambda new, old: jnp.where(position < mine, new, old), longer, running)

    return lax.fori_loop(0, count - 1, step, running)


def passed_along(block, axis, distance):
    devices = range(lax.axis_size(axis))
    route = [((i - distance) % len(devices), i) for i in devices]
    return lax.ppermute(block, axis, route)


def feature(u):
    return jnp.concatenate([jax.nn.softmax(u, axis=-1), jax.nn.softmax(-u, axis=-1)], axis=-1)


def add_pair(earlier, later):
    return (earlier[0] + later[0], earlier[1] + later[1])


def layer(final_results, gain, fquery, fkey, length, block_index):
    pairs, group, width = final_results.shape
    local_heads = fquery.shape[0]
    yf = final_results.astype(jnp.float32)
    squares = lax.psum(jnp.sum(yf * yf, axis=-1), "tp")
    normed = (
        yf * lax.rsqrt(squares / EMBED_DIMENSION + eps_norm)[:, :, None] * gain.astype(jnp.float32)
    ).astype(jnp.bfloat16)
    position = block_index * group + jnp.arange(group, dtype=jnp.int32)
    valid = (position[None, :] < length[:, None]).astype(jnp.float32)
    values = normed.reshape(pairs, group, local_heads, HEAD)
    query = feature(
        jnp.einsum("bchd,hdf->bchf", values, fquery, preferred_element_type=jnp.float32)
    ).astype(jnp.bfloat16)
    keys = (
        feature(jnp.einsum("bchd,hdf->bchf", values, fkey, preferred_element_type=jnp.float32))
        * valid[:, :, None, None]
    ).astype(jnp.bfloat16)
    local_state = jnp.einsum("bchf,bche->bhfe", keys, values, preferred_element_type=jnp.float32)
    local_zsum = jnp.sum(keys.astype(jnp.float32), axis=1)
    empty = (jnp.zeros_like(local_state), jnp.zeros_like(local_zsum))
    state, zsum = carried_in((local_state, local_zsum), "ctx", add_pair, empty)
    causal = (jnp.arange(group)[:, None] >= jnp.arange(group)[None, :]).astype(jnp.float32)
    scores_in = (
        jnp.einsum("bchf,bshf->bhcs", query, keys, preferred_element_type=jnp.float32) * causal
    )
    qf = query.astype(jnp.float32)
    den = jnp.sum(scores_in, axis=-1).transpose(0, 2, 1)
    den = den + jnp.einsum("bchf,bhf->bch", qf, zsum, precision=lax.Precision.HIGHEST)
    num = jnp.einsum(
        "bhcs,bshe->bche",
        scores_in.astype(jnp.bfloat16),
        values,
        preferred_element_type=jnp.float32,
    )
    num = num + jnp.einsum("bchf,bhfe->bche", qf, state, precision=lax.Precision.HIGHEST)
    attn = num / den[..., None]
    return ((yf + attn.reshape(pairs, group, width)) * valid[:, :, None]).astype(jnp.bfloat16)


def body(
    pending_activity,
    entry_rescale_vector,
    probe_lifting_matrices,
    lookup_lifting_matrices,
    usable_extents,
    payoff_readout_vector,
):
    block_index = lax.axis_index("ctx")
    final_results = pending_activity[0]
    length = usable_extents[0]
    final_results = layer(
        final_results,
        entry_rescale_vector[0, 0],
        probe_lifting_matrices[0, 0],
        lookup_lifting_matrices[0, 0],
        length,
        block_index,
    )
    group = final_results.shape[1]
    last = length - 1
    owner = last // group == block_index
    picker = (
        (jnp.arange(group, dtype=jnp.int32)[None, :] == (last % group)[:, None]) & owner[:, None]
    ).astype(jnp.bfloat16)
    rows = jnp.einsum("bc,bcd->bd", picker, final_results, preferred_element_type=jnp.float32)
    product = jnp.sum(rows * payoff_readout_vector.astype(jnp.float32), axis=-1)
    squares = jnp.sum(rows * rows, axis=-1)
    total, norm_total = lax.psum((product, squares), ("ctx", "tp"))
    found = total * lax.rsqrt(norm_total / EMBED_DIMENSION + eps_norm)
    handed = passed_along(final_results[None], "pipe", 1)
    return (handed, found[None])


def solution(mesh):
    placed = (
        P("pipe", None, "ctx", "tp"),
        P("pipe", None, "tp"),
        P("pipe", None, "tp", None, None),
        P("pipe", None, "tp", None, None),
        P("pipe", None),
        P("tp"),
    )
    return jax.shard_map(
        body,
        mesh=mesh,
        in_specs=placed,
        out_specs=(P("pipe", None, "ctx", "tp"), P("pipe", None)),
        check_vma=False,
    )
```

profile of v0, /device:TPU:1, one launch (start us, length us, event | category | flops | bytes accessed | tf_op | source)
XLA Modules:
  0.0 908.2 jit_solution(12916769631632735471)
XLA Ops:
  9.4 2.6 multiply_reduce_fusion
  12.0 9.0 psum.21
  31.2 63.7 %all-gather.1 = f32[512,128]{1,0:T(8,128)S(1)} all-gather(f32[32,128]{1,0:T(8,128)S(1)} %convert_reduce_fusion), channel_id=3, replica_groups=mesh['pipe'=16,'ctx'=16,'tp'=2] {'ctx'}, dimensions={0}, use_global_device_ids=true | all-gather | bytes 278528 | tf_op jit(solution)/shard_map/all_gather | solution.py:15
  100.6 659.7 %all-gather.4.cloned.1.call-done = f32[512,128,128]{2,1,0:T(8,128)} async-done(((f32[32,128,128]{2,1,0:T(8,128)}), f32[512,128,128]{2,1,0:T(8,128)}) %all-gather.4.cloned.1.call-update) | async-done | bytes 33554448 | tf_op jit(solution)/shard_map/all_gather | solution.py:15
  760.3 35.3 %while.16 = (s32[]{:T(128)}, f32[1,32,128,128]{3,2,1,0:T(8,128)S(1)}, f32[1,32,128]{2,1,0:T(8,128)S(1)}, s32[]{:T(128)}, f32[16,1,32,128,128]{4,3,2,1,0:T(8,128)...) while((s32[]{:T(128)}, f32[1,32,128,128]{3,2,1,0:T(8,128)S(1)}, ...), condition=%wide.region_12.13_spmd.clone, body=%wide.region_11.12_spmd.clone.sunk | while | flops 1585156 | bytes 6340723 | solution.py:24
  760.3 2.3 add_select_fusion.4
  762.6 2.3 add_select_fusion.4
  765.0 2.3 add_select_fusion.4
  767.3 2.3 add_select_fusion.4
  769.7 2.3 add_select_fusion.4
  772.0 2.3 add_select_fusion.4
  774.4 2.3 add_select_fusion.4
  776.8 2.3 add_select_fusion.4
  779.1 2.3 add_select_fusion.4
  781.5 2.3 add_select_fusion.4
  783.8 2.3 add_select_fusion.4
  786.2 2.3 add_select_fusion.4
  788.5 2.3 add_select_fusion.4
  790.9 2.3 add_select_fusion.4
  793.3 2.3 add_select_fusion.4
  801.4 3.6 multiply_convert_fusion
  805.6 2.2 collective-permute-start
  807.9 3.6 fusion.6
  812.7 85.4 %all-reduce = (f32[1]{0:T(128)}, f32[1]{0:T(128)}) all-reduce(f32[1]{0:T(128)} %bitcast.46, f32[1]{0:T(128)} %bitcast.47), channel_id=1, replica_groups=mesh['pipe'=16,'ctx'=16,'tp'=2] {'ctx','tp'}, use_global_device_ids=true, to_apply=%region_15.16 | all-reduce | flops 2 | bytes 16 | tf_op jit(solution)/shard_map/psum | solution.py:109
  (68 shorter events, 25.8 us)
Async XLA Ops:
  7.2 15.2 %copy-start = (bf16[1,1,32,128,64]{3,4,2,1,0:T(8,128)(2,1)S(1)}, bf16[1,1,32,128,64]{3,4,2,1,0:T(8,128)(2,1)}, u32[]{:S(2)}) copy-start(bf16[1,1,32,128,64]{3,4,2,1,0:T(8,128)(2,1)} %param.11) | copy-start | bytes 1572868
  7.2 4.8 copy-start.9
  7.2 753.1 %all-gather.4.cloned.1.call-start = ((), (), s32[]{:S(2)}) async-start(), calls=%async_computation | async-start | bytes 35651584 | tf_op jit(solution)/shard_map/all_gather | solution.py:15
  25.8 3.3 copy-start.1
  25.8 3.3 copy-start.2
  26.2 1.1 copy-start.5
  29.2 65.7 %copy-start.8 = (bf16[1,1,32,128,64]{3,4,2,1,0:T(8,128)(2,1)S(1)}, bf16[1,1,32,128,64]{3,4,2,1,0:T(8,128)(2,1)}, u32[]{:S(2)}) copy-start(bf16[1,1,32,128,64]{3,4,2,1,0:T(8,128)(2,1)} %param.10) | copy-start | bytes 1572868
  97.0 2.4 copy-start.6
  98.6 0.8 copy-start.4
  795.6 4.2 copy-start.7
  800.4 1.0 copy-start.3
  805.0 7.1 copy-start.10
  805.6 93.8 %collective-permute-start = (bf16[1,1,64,4096]{3,2,1,0:T(8,128)(2,1)S(1)}, bf16[1,1,64,4096]{3,2,1,0:T(8,128)(2,1)S(1)}, u32[]{:S(2)}, u32[]{:S(2)}) collective-permute-start(bf16[1,1,64,4096]{3,2,1,0:T(8,128)(2,1)S(1)} %copy.24), channel_id=1, source_target_pairs={{480,0},{0,32},{32,64},{64,96},{96,128},{128,160},{160,192},{192,2... | collective-permute-start | bytes 1572872 | tf_op jit(solution)/shard_map/ppermute | solution.py:30
Sparse Core Ops, SparseCore 0:
  29.2 730.9 all-gather.3
where the time goes:
time: 913 us; the launch traced here: 908 us
  waiting for transfers between devices  660 us (72%)
  blocking collectives  158 us (17%)
  other arithmetic  56 us (6%)
  between operations  17.5 us (2%)
  matrix products  9.96 us (1%)
    all_gather x1, waiting for transfers between devices, carried_in(): pieces = jax.tree.map(lambda part: lax.all_gather(part, axis), value)  660 us
    psum x1, blocking collectives, body(): total, norm_total = lax.psum((product, squares), ('ctx', 'tp'))  85.4 us
    all_gather x1, blocking collectives, carried_in(): pieces = jax.tree.map(lambda part: lax.all_gather(part, axis), value)  63.7 us
    select_n x30, other arithmetic, step(): jnp.where(position < mine, new, old)  34.9 us
  transfers between devices with their start and end apart: 2, of which 1 were waited for; matrix products, arithmetic and copies ran while one was open for 1% of the time, Pallas kernels for 0%

commit v1 on v0

v1 whole, which is shorter than its diff:
```python
import functools

import jax
import jax.numpy as jnp
from jax import lax
from jax.experimental import pallas as pl
from jax.experimental.pallas import tpu as pltpu
from jax.sharding import PartitionSpec as P

EMBED_DIMENSION = 8192
HEAD = 128
CHUNK = 256

eps_norm = 1e-05


def squares_kernel(y_ref, out_ref):
    total = jnp.zeros((y_ref.shape[0], 128), jnp.float32)
    for j in range(0, y_ref.shape[1], 128):
        part = y_ref[:, j : j + 128].astype(jnp.float32)
        total = total + part * part
    out_ref[...] = jnp.sum(total.T, axis=0, keepdims=True)


def norm_kernel(y_ref, squares_ref, gain_ref, out_ref):
    pieces, group, wide = out_ref.shape
    scale = lax.rsqrt(squares_ref[...] / EMBED_DIMENSION + eps_norm)
    scale = jnp.broadcast_to(scale, (128, group)).T
    for j in range(pieces):
        for i in range(0, wide, 128):
            at = j * wide + i
            part = y_ref[:, at : at + 128].astype(jnp.float32) * scale
            part = part * gain_ref[:, at : at + 128].astype(jnp.float32)
            out_ref[j, :, i : i + 128] = part.astype(jnp.bfloat16)


def feature(u):
    up = jnp.exp(u - jnp.max(u, axis=0, keepdims=True))
    down = jnp.exp(jnp.min(u, axis=0, keepdims=True) - u)
    up = up / jnp.sum(up, axis=0, keepdims=True)
    down = down / jnp.sum(down, axis=0, keepdims=True)
    return jnp.concatenate([up, down], axis=0)


def dot(a, b, dims):
    return lax.dot_general(a, b, (dims, ((), ())), preferred_element_type=jnp.float32)


def heads_kernel(where_ref, v_ref, probe_ref, lookup_ref, out_ref):
    length = where_ref[1]
    positions = v_ref.shape[0]
    causal = lax.broadcasted_iota(jnp.int32, (CHUNK, CHUNK), 0) >= lax.broadcasted_iota(
        jnp.int32, (CHUNK, CHUNK), 1
    )
    valid = (
        lax.broadcasted_iota(jnp.int32, (1, positions), 1) < length
    ).astype(jnp.float32)
    ones = jnp.ones((CHUNK, HEAD), jnp.bfloat16)
    for h in range(probe_ref.shape[0]):
        cols = slice(h * HEAD, (h + 1) * HEAD)
        v = v_ref[:, cols]
        query = feature(dot(probe_ref[h], v, ((0,), (1,)))).astype(jnp.bfloat16)
        keys = (feature(dot(lookup_ref[h], v, ((0,), (1,)))) * valid).astype(jnp.bfloat16)
        state = jnp.zeros((HEAD, 2 * HEAD), jnp.float32)
        for c in range(0, positions, CHUNK):
            q, k = query[:, c : c + CHUNK], keys[:, c : c + CHUNK]
            wide = jnp.concatenate([v[c : c + CHUNK], ones], axis=1)
            a = jnp.where(causal, dot(q, k, ((0,), (0,))), 0.0).astype(jnp.bfloat16)
            both = dot(a, wide, ((1,), (0,)))
            if c:
                high = state.astype(jnp.bfloat16)
                low = (state - high.astype(jnp.float32)).astype(jnp.bfloat16)
                both = both + dot(q, high, ((0,), (0,))) + dot(q, low, ((0,), (0,)))
            out_ref[c : c + CHUNK, cols] = (both[:, :HEAD] / both[:, HEAD:]).astype(jnp.bfloat16)
            if c + CHUNK < positions:
                state = state + dot(k, wide, ((1,), (0,)))


def join_kernel(where_ref, y_ref, attn_ref, readout_ref, out_ref, sums_ref):
    start, length = where_ref[0] * y_ref.shape[0], where_ref[1]
    pieces, group, wide = attn_ref.shape
    row = start + lax.broadcasted_iota(jnp.int32, (group, 128), 0)
    valid = (row < length).astype(jnp.float32)
    last = (row == length - 1).astype(jnp.float32)
    product = jnp.zeros((group, 128), jnp.float32)
    squares = jnp.zeros((group, 128), jnp.float32)
    for j in range(pieces):
        for i in range(0, wide, 128):
            at = j * wide + i
            part = y_ref[:, at : at + 128].astype(jnp.float32)
            part = (part + attn_ref[j, :, i : i + 128].astype(jnp.float32)) * valid
            part = part.astype(jnp.bfloat16)
            out_ref[:, at : at + 128] = part
            part = part.astype(jnp.float32) * last
            product = product + part * readout_ref[:, at : at + 128].astype(jnp.float32)
            squares = squares + part * part
    product = jnp.sum(jnp.sum(product, axis=0, keepdims=True), axis=1, keepdims=True)
    squares = jnp.sum(jnp.sum(squares, axis=0, keepdims=True), axis=1, keepdims=True)
    lane = lax.broadcasted_iota(jnp.int32, sums_ref.shape, 1)
    sums_ref[...] = jnp.where(lane == 0, product, jnp.where(lane == 1, squares, 0.0))


def passed_along(block, axis, distance):
    devices = range(lax.axis_size(axis))
    route = [((i - distance) % len(devices), i) for i in devices]
    return lax.ppermute(block, axis, route)


def vmem():
    return pl.BlockSpec(memory_space=pltpu.VMEM)


def smem():
    return pl.BlockSpec(memory_space=pltpu.SMEM)


def body(
    pending_activity,
    entry_rescale_vector,
    probe_lifting_matrices,
    lookup_lifting_matrices,
    usable_extents,
    payoff_readout_vector,
):
    blocks = lax.axis_size("ctx")
    group, width = pending_activity.shape[2:]
    heads = probe_lifting_matrices.shape[2]
    mine = heads // blocks
    wide = mine * HEAD
    positions = blocks * group
    y = pending_activity[0, 0]
    where = jnp.stack([lax.axis_index("ctx").astype(jnp.int32), usable_extents[0, 0]])

    squares = pl.pallas_call(
        squares_kernel,
        out_shape=jax.ShapeDtypeStruct((1, group), jnp.float32),
        in_specs=[vmem()],
        out_specs=vmem(),
    )(y)
    squares = lax.psum(squares, "tp")
    normed = pl.pallas_call(
        norm_kernel,
        out_shape=jax.ShapeDtypeStruct((blocks, group, wide), jnp.bfloat16),
        in_specs=[vmem()] * 3,
        out_specs=vmem(),
    )(y, squares, entry_rescale_vector[0])
    values = lax.all_to_all(normed, "ctx", split_axis=0, concat_axis=0, tiled=True)

    weights = pl.BlockSpec((mine, HEAD, HEAD // 2), lambda g, w: (w[0], 0, 0))
    whole = pl.BlockSpec((positions, wide), lambda g, w: (0, 0))
    attn = pl.pallas_call(
        heads_kernel,
        out_shape=jax.ShapeDtypeStruct((positions, wide), jnp.bfloat16),
        grid_spec=pltpu.PrefetchScalarGridSpec(
            num_scalar_prefetch=1,
            grid=(1,),
            in_specs=[whole, weights, weights],
            out_specs=whole,
        ),
        compiler_params=pltpu.CompilerParams(vmem_limit_bytes=32 * 1024 * 1024),
    )(where, values.reshape(positions, wide), probe_lifting_matrices[0, 0], lookup_lifting_matrices[0, 0])
    attn = lax.all_to_all(
        attn.reshape(blocks, group, wide), "ctx", split_axis=0, concat_axis=0, tiled=True
    )

    out, sums = pl.pallas_call(
        join_kernel,
        out_shape=(
            jax.ShapeDtypeStruct((group, width), jnp.bfloat16),
            jax.ShapeDtypeStruct((blocks, 128), jnp.float32),
        ),
        in_specs=[smem(), vmem(), vmem(), vmem()],
        out_specs=(vmem(), vmem()),
    )(where, y, attn, payoff_readout_vector[None])
    handed = passed_along(out[None, None], "pipe", 1)
    sums = lax.psum(sums, "tp")
    sums = jnp.sum(lax.all_to_all(sums, "ctx", split_axis=0, concat_axis=0, tiled=True), axis=0)
    found = sums[0] * lax.rsqrt(sums[1] / EMBED_DIMENSION + eps_norm)
    return (handed, found[None, None])


def solution(mesh):
    placed = (
        P("pipe", None, "ctx", "tp"),
        P("pipe", None, "tp"),
        P("pipe", None, "tp", None, None),
        P("pipe", None, "tp", None, None),
        P("pipe", None),
        P("tp"),
    )
    return jax.shard_map(
        body,
        mesh=mesh,
        in_specs=placed,
        out_specs=(P("pipe", None, "ctx", "tp"), P("pipe", None)),
        check_vma=False,
    )
```

time: 913 us -> 132 us (0.14)
  waiting for transfers between devices: 660 us -> 44.5 us
  blocking collectives: 158 us -> 42 us
  other arithmetic: 56 us -> 0.11 us
  starting transfers between devices: 2.25 us -> 24.2 us
  between operations: 17.5 us -> 3.83 us
  Pallas kernels: 0 us -> 10 us
  matrix products: 9.96 us -> 0 us
    all_gather x1 -> x0, waiting for transfers between devices: 660 us -> none  [carried_in(): pieces = jax.tree.map(lambda part: lax.all_gather(part, axis), value)]
    psum x2, blocking collectives: 94.4 us -> 16.3 us  [the longest x1 9.61 us: body(): squares = lax.psum(squares, 'tp')]
    all_gather x1 -> x0, blocking collectives: 63.7 us -> none  [carried_in(): pieces = jax.tree.map(lambda part: lax.all_gather(part, axis), value)]
    all_to_all x0 -> x2, waiting for transfers between devices: none -> 44.5 us  [the longest x1 25 us: body(): lax.all_to_all(normed, 'ctx', split_axis=0, concat_axis=0, tiled=True)]
    select_n x30 -> x0, other arithmetic: 34.9 us -> none  [step(): jnp.where(position < mine, new, old)]
    all_to_all x0 -> x1, blocking collectives: none -> 25.7 us  [body(): lax.all_to_all(sums, 'ctx', split_axis=0, concat_axis=0, tiled=True)]
    all_to_all x0 -> x2, starting transfers between devices: none -> 21 us  [the longest x1 12.1 us: body(): lax.all_to_all(normed, 'ctx', split_axis=0, concat_axis=0, tiled=True)]
    convert_element_type x7 -> x0, other arithmetic: 10.4 us -> none  [the longest x2 7.18 us: layer(): ((yf + attn.reshape(pairs, group, width)) * valid[:, :, None]).astype(jnp...]
  transfers between devices with their start and end apart: 2 -> 3, of which waited for: 1 -> 2; matrix products, arithmetic and copies ran while one was open for 1% -> 2% of each run, Pallas kernels for 0% -> 0%
where the time goes in v1:
time: 132 us; the launch traced here: 129 us
  waiting for transfers between devices  44.5 us (34%)
  blocking collectives  42 us (32%)
  starting transfers between devices  24.2 us (18%)
  Pallas kernels  10 us (8%)
  local copies, waits for them, and re-layouts  4.3 us (3%)
  between operations  3.83 us (3%)
    all_to_all x1, blocking collectives, body(): lax.all_to_all(sums, 'ctx', split_axis=0, concat_axis=0, tiled=True)  25.7 us
    all_to_all x1, waiting for transfers between devices, body(): lax.all_to_all(normed, 'ctx', split_axis=0, concat_axis=0, tiled=True)  25 us
    all_to_all x1, waiting for transfers between devices, body(): lax.all_to_all(attn.reshape(blocks, group, wide), 'ctx', split_axis=0, co...  19.6 us
    all_to_all x1, starting transfers between devices, body(): lax.all_to_all(normed, 'ctx', split_axis=0, concat_axis=0, tiled=True)  12.1 us
    psum x1, blocking collectives, body(): squares = lax.psum(squares, 'tp')  9.61 us
    all_to_all x1, starting transfers between devices, body(): lax.all_to_all(attn.reshape(blocks, group, wide), 'ctx', split_axis=0, co...  8.89 us
    psum x1, blocking collectives, body(): sums = lax.psum(sums, 'tp')  6.7 us
    pallas_call x1, Pallas kernels, body(): pl.pallas_call(heads_kernel, out_shape=jax.ShapeDtypeStruct((positions, w...  3.74 us
  transfers between devices with their start and end apart: 3, of which 2 were waited for; matrix products, arithmetic and copies ran while one was open for 2% of the time, Pallas kernels for 0%

profile of v1, /device:TPU:1, one launch (start us, length us, event | category | flops | bytes accessed | tf_op | source)
XLA Modules:
  0.0 129.1 jit_solution(1383266670558412424)
XLA Ops:
  0.6 1.8 %shard_map.77 = f32[1,64]{1,0:T(1,128)} custom-call(bf16[64,4096]{1,0:T(8,128)(2,1)} %bitcast.16), custom_call_target="tpu_custom_call" | custom-call | tf_op jit(solution)/shard_map/pallas_call | solution.py:134
  2.4 9.6 %psum.14.squares_ref = f32[1,64]{1,0:T(1,128)} all-reduce(f32[1,64]{1,0:T(1,128)} %shard_map.77), channel_id=1, replica_groups=mesh['pipe'=16,'ctx'=16,'tp'=2] {'tp'}, use_global_device_ids=true, to_apply=%region_0.0 | all-reduce | flops 64 | bytes 512 | tf_op jit(solution)/shard_map/psum | solution.py:140
  12.0 2.1 %shard_map.78 = bf16[16,64,256]{2,1,0:T(8,128)(2,1)} custom-call(bf16[64,4096]{1,0:T(8,128)(2,1)} %bitcast.17, f32[1,64]{1,0:T(1,128)} %psum.14.squares_ref, bf16[1,4096]{1,0:T(2,128)(2,1)} %bitcast.20), custom_call_target="tpu_custom_call" | custom-call | tf_op jit(solution)/shard_map/pallas_call | solution.py:141
  14.1 12.1 %all-to-all-start = ((bf16[16,64,256]{2,1,0:T(8,128)(2,1)}), bf16[16,64,256]{2,1,0:T(8,128)(2,1)S(1)}, u32[]{:S(2)}, u32[]{:S(2)}) async-start(bf16[16,64,256]{2,1,0:T(8,128)(2,1)} %shard_map.78), calls=%async_computation | async-start | bytes 1048576 | tf_op jit(solution)/shard_map/all_to_all | solution.py:147
  26.9 0.0 copy-done.2
  26.9 0.0 copy-start.3
  26.9 0.5 copy.10
  27.4 0.5 copy-done.3
  27.9 0.5 copy.11
  28.4 0.1 pad_add_fusion.where_ref
  28.5 25.0 %all-to-all-done = bf16[16,64,256]{2,1,0:T(8,128)(2,1)S(1)} async-done(((bf16[16,64,256]{2,1,0:T(8,128)(2,1)}), bf16[16,64,256]{2,1,0:T(8,128)(2,1)S(1)}, u32[]{:S(2)}, u32[]{:S(2)}) %all-to-all-start) | async-done | bytes 524320 | tf_op jit(solution)/shard_map/all_to_all | solution.py:147
  53.4 0.0 copy-done
  53.5 3.7 %shard_map.79 = bf16[1024,256]{1,0:T(8,128)(2,1)} custom-call(s32[2]{0:T(128)S(1)} %pad_add_fusion.where_ref, bf16[1024,256]{1,0:T(8,128)(2,1)S(1)} %bitcast.15, bf16[32,128,64]{2,1,0:T(8,128)(2,1)S(1)} %bitcast.13, bf16[32,128,64]{2,1,0:T(8,128)(2,1)S(1)} %bitcast.14), custom_call_target="tpu_custom_call" | custom-call | tf_op jit(solution)/shard_map/pallas_call | solution.py:151
  57.2 8.9 %all-to-all-start.1 = ((bf16[16,64,256]{2,1,0:T(8,128)(2,1)}), bf16[16,64,256]{2,1,0:T(8,128)(2,1)S(1)}, u32[]{:S(2)}, u32[]{:S(2)}) async-start(bf16[16,64,256]{2,1,0:T(8,128)(2,1)} %bitcast.7), calls=%async_computation.1 | async-start | bytes 1048576 | tf_op jit(solution)/shard_map/all_to_all | solution.py:162
  66.1 0.6 broadcast_in_dim.9.readout_ref
  66.7 19.6 %all-to-all-done.1.attn_ref = bf16[16,64,256]{2,1,0:T(8,128)(2,1)S(1)} async-done(((bf16[16,64,256]{2,1,0:T(8,128)(2,1)}), bf16[16,64,256]{2,1,0:T(8,128)(2,1)S(1)}, u32[]{:S(2)}, u32[]{:S(2)}) %all-to-all-start.1) | async-done | bytes 524320 | tf_op jit(solution)/shard_map/all_to_all | solution.py:162
  86.3 0.8 copy-done.1
  87.1 2.5 %shard_map.80 = (bf16[64,4096]{1,0:T(8,128)(2,1)}, f32[16,128]{1,0:T(8,128)}) custom-call(s32[2]{0:T(128)} %copy-done, bf16[64,4096]{1,0:T(8,128)(2,1)} %bitcast.18, bf16[16,64,256]{2,1,0:T(8,128)(2,1)} %copy-done.1, bf16[1,4096]{1,0:T(2,128)(2,1)} %broadcast_in_dim.9.readout_ref), custom_call_target="tpu_custom_call" | custom-call | tf_op jit(solution)/shard_map/pallas_call | solution.py:166
  89.6 3.2 %collective-permute-start = (bf16[1,1,64,4096]{3,2,1,0:T(8,128)(2,1)}, bf16[1,1,64,4096]{3,2,1,0:T(8,128)(2,1)S(1)}, u32[]{:S(2)}, u32[]{:S(2)}) collective-permute-start(bf16[1,1,64,4096]{3,2,1,0:T(8,128)(2,1)} %bitcast.22), channel_id=1, source_target_pairs={{480,0},{0,32},{32,64},{64,96},{96,128},{128,160},{160,192},{192,2... | collective-permute-start | bytes 1572872 | tf_op jit(solution)/shard_map/ppermute | solution.py:106
  92.8 6.7 %psum.15 = f32[16,1,128]{2,0,1:T(8,128)S(1)} all-reduce(f32[16,1,128]{2,0,1:T(8,128)} %bitcast.21), channel_id=1, replica_groups=mesh['pipe'=16,'ctx'=16,'tp'=2] {'tp'}, use_global_device_ids=true, to_apply=%region_1.0 | all-reduce | flops 2048 | bytes 16384 | tf_op jit(solution)/shard_map/psum | solution.py:176
  99.5 25.7 %all_to_all.19 = f32[16,1,128]{2,1,0:T(1,128)S(1)} all-to-all(f32[16,1,128]{2,1,0:T(1,128)S(1)} %bitcast.19), channel_id=1, replica_groups=mesh['pipe'=16,'ctx'=16,'tp'=2] {'ctx'}, dimensions={0} | all-to-all | bytes 16384 | tf_op jit(solution)/shard_map/all_to_all | solution.py:177
  125.2 0.6 fusion
  127.1 0.0 collective-permute-done
  127.1 0.8 copy.15
  (6 shorter events, 0.0 us)
Async XLA Ops:
  14.1 12.8 %copy-start.2 = (bf16[1,1,32,128,64]{3,4,2,1,0:T(8,128)(2,1)S(1)}, bf16[1,1,32,128,64]{3,4,2,1,0:T(8,128)(2,1)}, u32[]{:S(2)}) copy-start(bf16[1,1,32,128,64]{3,4,2,1,0:T(8,128)(2,1)} %param.8) | copy-start | bytes 1572868
  14.1 39.4 %all-to-all-start = ((bf16[16,64,256]{2,1,0:T(8,128)(2,1)}), bf16[16,64,256]{2,1,0:T(8,128)(2,1)S(1)}, u32[]{:S(2)}, u32[]{:S(2)}) async-start(bf16[16,64,256]{2,1,0:T(8,128)(2,1)} %shard_map.78), calls=%async_computation | async-start | bytes 1048576 | tf_op jit(solution)/shard_map/all_to_all | solution.py:147
  26.9 1.0 copy-start.3
  28.5 25.0 %copy-start = (s32[2]{0:T(128)}, s32[2]{0:T(128)S(1)}, u32[]{:S(2)}) copy-start(s32[2]{0:T(128)S(1)} %pad_add_fusion.where_ref) | copy-start | bytes 28
  57.2 8.9 %copy-start.4 = (bf16[4096]{0:T(1024)(128)(2,1)S(1)}, bf16[4096]{0:T(1024)(128)(2,1)}, u32[]{:S(2)}) copy-start(bf16[4096]{0:T(1024)(128)(2,1)} %param.11) | copy-start | bytes 24580
  57.2 29.1 %all-to-all-start.1 = ((bf16[16,64,256]{2,1,0:T(8,128)(2,1)}), bf16[16,64,256]{2,1,0:T(8,128)(2,1)S(1)}, u32[]{:S(2)}, u32[]{:S(2)}) async-start(bf16[16,64,256]{2,1,0:T(8,128)(2,1)} %bitcast.7), calls=%async_computation.1 | async-start | bytes 1048576 | tf_op jit(solution)/shard_map/all_to_all | solution.py:162
  86.3 0.8 copy-start.1
  89.6 37.6 %collective-permute-start = (bf16[1,1,64,4096]{3,2,1,0:T(8,128)(2,1)}, bf16[1,1,64,4096]{3,2,1,0:T(8,128)(2,1)S(1)}, u32[]{:S(2)}, u32[]{:S(2)}) collective-permute-start(bf16[1,1,64,4096]{3,2,1,0:T(8,128)(2,1)} %bitcast.22), channel_id=1, source_target_pairs={{480,0},{0,32},{32,64},{64,96},{96,128},{128,160},{160,192},{192,2... | collective-permute-start | bytes 1572872 | tf_op jit(solution)/shard_map/ppermute | solution.py:106

commit v2 on v1

v2 whole, which is shorter than its diff:
```python
import jax
import jax.numpy as jnp
from jax import lax
from jax.experimental import pallas as pl
from jax.experimental.pallas import tpu as pltpu
from jax.sharding import PartitionSpec as P

EMBED_DIMENSION = 8192
HEAD = 128
SPLIT = 4
EXTRA = 8

eps_norm = 1e-05


def three(value):
    parts = []
    for _ in range(3):
        parts.append(value.astype(jnp.bfloat16).astype(jnp.float32))
        value = value - parts[-1]
    return parts


def cut_kernel(y_ref, pieces_ref):
    blocks, group = pieces_ref.shape[0], y_ref.shape[0]
    heads = y_ref.shape[1] // HEAD // blocks
    total = jnp.zeros((group, HEAD), jnp.float32)
    for j in range(blocks):
        for h in range(heads):
            cols = slice((j * heads + h) * HEAD, (j * heads + h + 1) * HEAD)
            part = y_ref[:, cols]
            pieces_ref[j, h * group : (h + 1) * group, :] = part
            part = part.astype(jnp.float32)
            total = total + part * part
    total = jnp.concatenate([total, jnp.zeros((HEAD - group, HEAD), jnp.float32)], axis=0)
    total = jnp.sum(total.T, axis=0, keepdims=True)
    rows = three(total) + [jnp.zeros((EXTRA - 3, HEAD), jnp.float32)]
    rows = jnp.concatenate(rows, axis=0).astype(jnp.bfloat16)
    for j in range(blocks):
        pieces_ref[j, heads * group :, :] = rows


def feature(u):
    up = jnp.exp(u - jnp.max(u, axis=0, keepdims=True))
    down = jnp.exp(jnp.min(u, axis=0, keepdims=True) - u)
    up = up * (1.0 / jnp.sum(up, axis=0, keepdims=True))
    down = down * (1.0 / jnp.sum(down, axis=0, keepdims=True))
    return jnp.concatenate([up, down], axis=0)


def dot(a, b, dims):
    return lax.dot_general(a, b, (dims, ((), ())), preferred_element_type=jnp.float32)


def heads_kernel(
    where_ref, y_ref, squares_ref, gain_ref, probe_ref, lookup_ref, readout_ref, out_ref
):
    length = where_ref[1]
    blocks, heads = y_ref.shape[0], probe_ref.shape[0]
    group = (y_ref.shape[1] - EXTRA) // heads
    lines = blocks // SPLIT
    positions, chunk = blocks * group, SPLIT * group
    causal = lax.broadcasted_iota(jnp.int32, (chunk, chunk), 0) >= lax.broadcasted_iota(
        jnp.int32, (chunk, chunk), 1
    )
    at = lax.broadcasted_iota(jnp.int32, (chunk, HEAD), 0)
    valid = (lax.broadcasted_iota(jnp.int32, (1, positions), 1) < length).astype(jnp.float32)
    ones = jnp.ones((chunk, HEAD), jnp.bfloat16)
    scales = []
    for j in range(blocks):
        row = squares_ref[j : j + 1, :group]
        scale = lax.rsqrt(row / EMBED_DIMENSION + eps_norm)
        scales.append(jnp.broadcast_to(scale, (HEAD, group)).T)
    product = jnp.zeros((1, 1), jnp.float32)
    squares = jnp.zeros((1, 1), jnp.float32)
    for h in range(heads):
        rows = slice(h * group, (h + 1) * group)
        y = [y_ref[j, rows, :].astype(jnp.float32) for j in range(blocks)]
        gain = gain_ref[h].astype(jnp.float32)
        v = [(y[j] * scales[j] * gain).astype(jnp.bfloat16) for j in range(blocks)]
        v = jnp.concatenate(v, axis=0)
        query = feature(dot(probe_ref[h], v, ((0,), (1,)))).astype(jnp.bfloat16)
        keys = (feature(dot(lookup_ref[h], v, ((0,), (1,)))) * valid).astype(jnp.bfloat16)
        state = jnp.zeros((HEAD, 2 * HEAD), jnp.float32)
        last = jnp.zeros((1, HEAD), jnp.float32)
        for x in range(lines):
            cut = slice(x * chunk, (x + 1) * chunk)
            q, k = query[:, cut], keys[:, cut]
            wide = jnp.concatenate([v[cut], ones], axis=1)
            a = jnp.where(causal, dot(q, k, ((0,), (0,))), 0.0).astype(jnp.bfloat16)
            both = dot(a, wide, ((1,), (0,)))
            if x:
                high = state.astype(jnp.bfloat16)
                low = (state - high.astype(jnp.float32)).astype(jnp.bfloat16)
                both = both + dot(q, high, ((0,), (0,))) + dot(q, low, ((0,), (0,)))
            out = both[:, :HEAD] / both[:, HEAD:]
            out = out + jnp.concatenate(y[x * SPLIT : (x + 1) * SPLIT], axis=0)
            out = jnp.where(at < length - x * chunk, out, 0.0).astype(jnp.bfloat16)
            for z in range(SPLIT):
                out_ref[x * SPLIT + z, rows, :] = out[z * group : (z + 1) * group]
            out = jnp.where(at == length - 1 - x * chunk, out.astype(jnp.float32), 0.0)
            last = last + jnp.sum(out, axis=0, keepdims=True)
            if x + 1 < lines:
                state = state + dot(k, wide, ((1,), (0,)))
        product = product + jnp.sum(last * readout_ref[h].astype(jnp.float32), axis=1, keepdims=True)
        squares = squares + jnp.sum(last * last, axis=1, keepdims=True)
    lane = lax.broadcasted_iota(jnp.int32, (EXTRA, HEAD), 1)
    sums = jnp.zeros((EXTRA, HEAD), jnp.float32)
    for n, part in enumerate(three(product) + three(squares)):
        sums = jnp.where(lane == n, part, sums)
    for j in range(blocks):
        out_ref[j, heads * group :, :] = sums.astype(jnp.bfloat16)


def vmem():
    return pl.BlockSpec(memory_space=pltpu.VMEM)


def body(
    pending_activity,
    entry_rescale_vector,
    probe_lifting_matrices,
    lookup_lifting_matrices,
    usable_extents,
    payoff_readout_vector,
):
    blocks, sections = lax.axis_size("ctx"), lax.axis_size("pipe")
    group, width = pending_activity.shape[2:]
    y = pending_activity[0, 0]
    probe, lookup = probe_lifting_matrices[0, 0], lookup_lifting_matrices[0, 0]
    heads = probe.shape[0] // blocks
    readout = payoff_readout_vector.reshape(-1, 1, HEAD)
    gain = entry_rescale_vector.reshape(-1, 1, HEAD)
    where = jnp.stack([lax.axis_index("ctx").astype(jnp.int32), usable_extents[0, 0]])

    shape = (blocks, heads * group + EXTRA, HEAD)
    pieces = pl.pallas_call(
        cut_kernel,
        out_shape=jax.ShapeDtypeStruct(shape, jnp.bfloat16),
        in_specs=[vmem()],
        out_specs=vmem(),
    )(y)
    pieces = lax.all_to_all(pieces, "ctx", split_axis=0, concat_axis=0, tiled=True)
    squares = jnp.sum(pieces[:, heads * group : heads * group + 3, :].astype(jnp.float32), axis=1)
    squares = lax.psum(squares, "tp")

    def mine(*tail):
        return pl.BlockSpec((heads, *tail), lambda g, w: (w[0], *(0 for _ in tail)))

    def whole(*shape):
        return pl.BlockSpec(shape, lambda g, w: (0,) * len(shape))

    weights = mine(HEAD, HEAD // 2)
    out = pl.pallas_call(
        heads_kernel,
        out_shape=jax.ShapeDtypeStruct(shape, jnp.bfloat16),
        grid_spec=pltpu.PrefetchScalarGridSpec(
            num_scalar_prefetch=1,
            grid=(1,),
            in_specs=[
                whole(*shape),
                whole(*squares.shape),
                mine(1, HEAD),
                weights,
                weights,
                mine(1, HEAD),
            ],
            out_specs=whole(*shape),
        ),
        compiler_params=pltpu.CompilerParams(vmem_limit_bytes=32 * 1024 * 1024),
    )(where, pieces, squares, gain, probe, lookup, readout)
    out = lax.all_to_all(out, "ctx", split_axis=0, concat_axis=0, tiled=True)
    sums = jnp.sum(out[:, heads * group, :].astype(jnp.float32), axis=0)
    handed = lax.ppermute(out, "pipe", [(p, (p + 1) % sections) for p in range(sections)])
    handed = handed[:, : heads * group].reshape(blocks, heads, group, HEAD)
    handed = handed.transpose(2, 0, 1, 3).reshape(group, width)
    sums = lax.psum(sums, "tp")
    found = jnp.sum(sums[:3]) * lax.rsqrt(jnp.sum(sums[3:6]) / EMBED_DIMENSION + eps_norm)
    return (handed[None, None], found[None, None])


def solution(mesh):
    placed = (
        P("pipe", None, "ctx", "tp"),
        P("pipe", None, "tp"),
        P("pipe", None, "tp", None, None),
        P("pipe", None, "tp", None, None),
        P("pipe", None),
        P("tp"),
    )
    return jax.shard_map(
        body,
        mesh=mesh,
        in_specs=placed,
        out_specs=(P("pipe", None, "ctx", "tp"), P("pipe", None)),
        check_vma=False,
    )
```

time: 132 us -> 122 us (0.924)
  the two profiles are of different devices: /device:TPU:1 before, /device:TPU:32 now
where the time goes in v2:
time: 122 us
  blocking collectives  44.9 us (37%)
  waiting for transfers between devices  43.1 us (35%)
  starting transfers between devices  20.4 us (17%)
  Pallas kernels  5.21 us (4%)
  between operations  3.85 us (3%)
  local copies, waits for them, and re-layouts  3.34 us (3%)
    all_to_all x1, blocking collectives, body(): out = lax.all_to_all(out, 'ctx', split_axis=0, concat_axis=0, tiled=True)  40 us
    all_to_all x1, waiting for transfers between devices, body(): lax.all_to_all(pieces, 'ctx', split_axis=0, concat_axis=0, tiled=True)  33 us
    all_to_all x1, starting transfers between devices, body(): lax.all_to_all(pieces, 'ctx', split_axis=0, concat_axis=0, tiled=True)  16.9 us
    ppermute x1, waiting for transfers between devices, body(): lax.ppermute(out, 'pipe', [(p, (p + 1) % sections) for p in range(section...  10 us
    ppermute x1, starting transfers between devices, body(): lax.ppermute(out, 'pipe', [(p, (p + 1) % sections) for p in range(section...  3.47 us
    pallas_call x1, Pallas kernels, body(): pl.pallas_call(heads_kernel, out_shape=jax.ShapeDtypeStruct(shape, jnp.bf...  3.09 us
    psum x1, blocking collectives, body(): squares = lax.psum(squares, 'tp')  2.5 us
    psum x1, blocking collectives, body(): sums = lax.psum(sums, 'tp')  2.46 us
  transfers between devices with their start and end apart: 2, of which 2 were waited for; matrix products, arithmetic and copies ran while one was open for 1% of the time, Pallas kernels for 0%

profile of v2, /device:TPU:32, one launch (start us, length us, event | category | flops | bytes accessed | tf_op | source)
XLA Modules:
  0.0 121.6 jit_solution(17814985805552027178)
XLA Ops:
  0.6 2.1 %shard_map.77 = bf16[16,136,128]{2,1,0:T(8,128)(2,1)} custom-call(bf16[64,4096]{1,0:T(8,128)(2,1)} %bitcast.16), custom_call_target="tpu_custom_call" | custom-call | tf_op jit(solution)/shard_map/pallas_call | solution.py:137
  2.7 0.0 copy-start.1
  2.7 16.9 %all-to-all-start = ((bf16[16,136,128]{2,1,0:T(8,128)(2,1)}), bf16[16,136,128]{2,1,0:T(8,128)(2,1)S(1)}, u32[]{:S(2)}, u32[]{:S(2)}) async-start(bf16[16,136,128]{2,1,0:T(8,128)(2,1)} %shard_map.77), calls=%async_computation | async-start | bytes 1114112 | tf_op jit(solution)/shard_map/all_to_all | solution.py:143
  19.6 0.0 copy-start.3
  20.3 0.0 copy-done.3
  20.4 0.0 copy-done.1
  20.4 0.0 copy-start.2
  20.4 0.5 copy.11
  20.9 0.5 copy-done.2
  21.4 0.5 copy.12
  21.9 0.1 pad_add_fusion.where_ref
  22.0 33.0 %all-to-all-done.y_ref = bf16[16,136,128]{2,1,0:T(8,128)(2,1)S(1)} async-done(((bf16[16,136,128]{2,1,0:T(8,128)(2,1)}), bf16[16,136,128]{2,1,0:T(8,128)(2,1)S(1)}, u32[]{:S(2)}, u32[]{:S(2)}) %all-to-all-start) | async-done | bytes 557088 | tf_op jit(solution)/shard_map/all_to_all | solution.py:143
  55.0 0.0 copy-start
  55.1 2.5 %psum.14.squares_ref = f32[16,128]{1,0:T(8,128)S(1)} all-reduce(f32[16,128]{1,0:T(8,128)S(1)} %convert_reduce_fusion), channel_id=1, replica_groups=mesh['pipe'=16,'ctx'=16,'tp'=2] {'tp'}, use_global_device_ids=true, to_apply=%region_1.0 | all-reduce | flops 2048 | bytes 16384 | tf_op jit(solution)/shard_map/psum | solution.py:145
  57.6 0.0 copy-done
  57.6 3.1 %shard_map.78 = bf16[16,136,128]{2,1,0:T(8,128)(2,1)S(1)} custom-call(s32[2]{0:T(128)S(1)} %pad_add_fusion.where_ref, bf16[16,136,128]{2,1,0:T(8,128)(2,1)S(1)} %all-to-all-done.y_ref, f32[16,128]{1,0:T(8,128)S(1)} %psum.14.squares_ref, bf16[32,1,128]{2,1,0:T(2,128)(2,1)S(1)} %bitcast.14, bf16[32,128,64]{2,1,0:T(8,128)(2,1)S(1)} %bitcast.12, ...), custom_call_target="tpu_custom_call" | custom-call | tf_op jit(solution)/shard_map/pallas_call | solution.py:154
  60.7 40.0 %all_to_all.10 = bf16[16,136,128]{2,1,0:T(8,128)(2,1)S(1)} all-to-all(bf16[16,136,128]{2,1,0:T(8,128)(2,1)S(1)} %shard_map.78), channel_id=1, replica_groups=mesh['pipe'=16,'ctx'=16,'tp'=2] {'ctx'}, dimensions={0} | all-to-all | bytes 1114112 | tf_op jit(solution)/shard_map/all_to_all | solution.py:172
  100.6 3.5 %collective-permute-start = (bf16[16,136,128]{2,1,0:T(8,128)(2,1)S(1)}, bf16[16,136,128]{2,1,0:T(8,128)(2,1)S(1)}, u32[]{:S(2)}, u32[]{:S(2)}) collective-permute-start(bf16[16,136,128]{2,1,0:T(8,128)(2,1)S(1)} %all_to_all.10), channel_id=1, source_target_pairs={{0,32},{32,64},{64,96},{96,128},{128,160},{160,192},{192,224},{224... | collective-permute-start | bytes 1671176 | tf_op jit(solution)/shard_map/ppermute | solution.py:174
  104.1 2.5 %psum.15 = f32[128]{0:T(128)S(1)} all-reduce(f32[128]{0:T(128)S(1)} %fusion), channel_id=1, replica_groups=mesh['pipe'=16,'ctx'=16,'tp'=2] {'tp'}, use_global_device_ids=true, to_apply=%region_3.0 | all-reduce | flops 128 | bytes 1024 | tf_op jit(solution)/shard_map/psum | solution.py:177
  106.6 0.7 slice_reduce_fusion
  108.6 10.0 %collective-permute-done = bf16[16,136,128]{2,1,0:T(8,128)(2,1)S(1)} collective-permute-done((bf16[16,136,128]{2,1,0:T(8,128)(2,1)S(1)}, bf16[16,136,128]{2,1,0:T(8,128)(2,1)S(1)}, u32[]{:S(2)}, u32[]{:S(2)}) %collective-permute-start) | collective-permute-done | bytes 557088 | tf_op jit(solution)/shard_map/ppermute | solution.py:174
  118.7 0.5 copy.14
  119.3 1.2 broadcast_in_dim_reshape.3
  (4 shorter events, 0.1 us)
Async XLA Ops:
  2.7 17.6 %copy-start.1 = (bf16[1,1,32,128,64]{3,4,2,1,0:T(8,128)(2,1)S(1)}, bf16[1,1,32,128,64]{3,4,2,1,0:T(8,128)(2,1)}, u32[]{:S(2)}) copy-start(bf16[1,1,32,128,64]{3,4,2,1,0:T(8,128)(2,1)} %param.8) | copy-start | bytes 1572868
  2.7 52.3 %all-to-all-start = ((bf16[16,136,128]{2,1,0:T(8,128)(2,1)}), bf16[16,136,128]{2,1,0:T(8,128)(2,1)S(1)}, u32[]{:S(2)}, u32[]{:S(2)}) async-start(bf16[16,136,128]{2,1,0:T(8,128)(2,1)} %shard_map.77), calls=%async_computation | async-start | bytes 1114112 | tf_op jit(solution)/shard_map/all_to_all | solution.py:143
  19.6 0.7 copy-start.3
  20.4 1.0 copy-start.2
  55.0 2.5 %copy-start = (bf16[1,1,4096]{2,1,0:T(2,128)(2,1)S(1)}, bf16[1,1,4096]{2,1,0:T(2,128)(2,1)}, u32[]{:S(2)}) copy-start(bf16[1,1,4096]{2,1,0:T(2,128)(2,1)} %param.7) | copy-start | bytes 24580
  100.6 18.0 %collective-permute-start = (bf16[16,136,128]{2,1,0:T(8,128)(2,1)S(1)}, bf16[16,136,128]{2,1,0:T(8,128)(2,1)S(1)}, u32[]{:S(2)}, u32[]{:S(2)}) collective-permute-start(bf16[16,136,128]{2,1,0:T(8,128)(2,1)S(1)} %all_to_all.10), channel_id=1, source_target_pairs={{0,32},{32,64},{64,96},{96,128},{128,160},{160,192},{192,224},{224... | collective-permute-start | bytes 1671176 | tf_op jit(solution)/shard_map/ppermute | solution.py:174

commit v3 on v2

--- a/solution.py
+++ b/solution.py
@@ -13,6 +13,11 @@
 eps_norm = 1e-05
 
 
+def ordered(blocks):
+    lines, far = blocks // SPLIT, SPLIT // 2
+    return [x * SPLIT + z + far * n for z in range(far) for x in range(lines) for n in range(2)]
+
+
 def three(value):
     parts = []
     for _ in range(3):
@@ -25,11 +30,11 @@
     blocks, group = pieces_ref.shape[0], y_ref.shape[0]
     heads = y_ref.shape[1] // HEAD // blocks
     total = jnp.zeros((group, HEAD), jnp.float32)
-    for j in range(blocks):
+    for n, j in enumerate(ordered(blocks)):
         for h in range(heads):
             cols = slice((j * heads + h) * HEAD, (j * heads + h + 1) * HEAD)
             part = y_ref[:, cols]
-            pieces_ref[j, h * group : (h + 1) * group, :] = part
+            pieces_ref[n, h * group : (h + 1) * group, :] = part
             part = part.astype(jnp.float32)
             total = total + part * part
     total = jnp.concatenate([total, jnp.zeros((HEAD - group, HEAD), jnp.float32)], axis=0)
@@ -53,10 +58,10 @@
 
 
 def heads_kernel(
-    where_ref, y_ref, squares_ref, gain_ref, probe_ref, lookup_ref, readout_ref, out_ref
+    length_ref, y_ref, squares_ref, gain_ref, lifting_ref, readout_ref, out_ref
 ):
-    length = where_ref[1]
-    blocks, heads = y_ref.shape[0], probe_ref.shape[0]
+    length = length_ref[0, 0]
+    blocks, heads = y_ref.shape[0], lifting_ref.shape[0]
     group = (y_ref.shape[1] - EXTRA) // heads
     lines = blocks // SPLIT
     positions, chunk = blocks * group, SPLIT * group
@@ -66,21 +71,24 @@
     at = lax.broadcasted_iota(jnp.int32, (chunk, HEAD), 0)
     valid = (lax.broadcasted_iota(jnp.int32, (1, positions), 1) < length).astype(jnp.float32)
     ones = jnp.ones((chunk, HEAD), jnp.bfloat16)
+    order = ordered(blocks)
+    place = [order.index(j) for j in range(blocks)]
     scales = []
     for j in range(blocks):
-        row = squares_ref[j : j + 1, :group]
+        row = squares_ref[place[j] : place[j] + 1, :group]
         scale = lax.rsqrt(row / EMBED_DIMENSION + eps_norm)
         scales.append(jnp.broadcast_to(scale, (HEAD, group)).T)
     product = jnp.zeros((1, 1), jnp.float32)
     squares = jnp.zeros((1, 1), jnp.float32)
     for h in range(heads):
         rows = slice(h * group, (h + 1) * group)
-        y = [y_ref[j, rows, :].astype(jnp.float32) for j in range(blocks)]
-        gain = gain_ref[h].astype(jnp.float32)
+        y = [y_ref[place[j], rows, :].astype(jnp.float32) for j in range(blocks)]
+        gain = gain_ref[h : h + 1, :].astype(jnp.float32)
         v = [(y[j] * scales[j] * gain).astype(jnp.bfloat16) for j in range(blocks)]
         v = jnp.concatenate(v, axis=0)
-        query = feature(dot(probe_ref[h], v, ((0,), (1,)))).astype(jnp.bfloat16)
-        keys = (feature(dot(lookup_ref[h], v, ((0,), (1,)))) * valid).astype(jnp.bfloat16)
+        u = dot(lifting_ref[h], v, ((1,), (1,)))
+        query = feature(u[: HEAD // 2]).astype(jnp.bfloat16)
+        keys = (feature(u[HEAD // 2 :]) * valid).astype(jnp.bfloat16)
         state = jnp.zeros((HEAD, 2 * HEAD), jnp.float32)
         last = jnp.zeros((1, HEAD), jnp.float32)
         for x in range(lines):
@@ -97,12 +105,12 @@
             out = out + jnp.concatenate(y[x * SPLIT : (x + 1) * SPLIT], axis=0)
             out = jnp.where(at < length - x * chunk, out, 0.0).astype(jnp.bfloat16)
             for z in range(SPLIT):
-                out_ref[x * SPLIT + z, rows, :] = out[z * group : (z + 1) * group]
+                out_ref[place[x * SPLIT + z], rows, :] = out[z * group : (z + 1) * group]
             out = jnp.where(at == length - 1 - x * chunk, out.astype(jnp.float32), 0.0)
             last = last + jnp.sum(out, axis=0, keepdims=True)
             if x + 1 < lines:
                 state = state + dot(k, wide, ((1,), (0,)))
-        product = product + jnp.sum(last * readout_ref[h].astype(jnp.float32), axis=1, keepdims=True)
+        product = product + jnp.sum(last * readout_ref[h : h + 1, :].astype(jnp.float32), axis=1, keepdims=True)
         squares = squares + jnp.sum(last * last, axis=1, keepdims=True)
     lane = lax.broadcasted_iota(jnp.int32, (EXTRA, HEAD), 1)
     sums = jnp.zeros((EXTRA, HEAD), jnp.float32)
@@ -110,6 +118,17 @@
         sums = jnp.where(lane == n, part, sums)
     for j in range(blocks):
         out_ref[j, heads * group :, :] = sums.astype(jnp.bfloat16)
+
+
+def exchanged(pieces):
+    return lax.all_to_all(
+        pieces,
+        "ctx",
+        split_axis=0,
+        concat_axis=0,
+        axis_index_groups=[ordered(lax.axis_size("ctx"))],
+        tiled=True,
+    )
 
 
 def vmem():
@@ -129,9 +148,11 @@
     y = pending_activity[0, 0]
     probe, lookup = probe_lifting_matrices[0, 0], lookup_lifting_matrices[0, 0]
     heads = probe.shape[0] // blocks
-    readout = payoff_readout_vector.reshape(-1, 1, HEAD)
-    gain = entry_rescale_vector.reshape(-1, 1, HEAD)
-    where = jnp.stack([lax.axis_index("ctx").astype(jnp.int32), usable_extents[0, 0]])
+    first = lax.axis_index("ctx") * heads
+    lifting = jnp.concatenate([probe.swapaxes(1, 2), lookup.swapaxes(1, 2)], axis=1)
+    lifting = lax.dynamic_slice_in_dim(lifting, first, heads)
+    gain = lax.dynamic_slice_in_dim(entry_rescale_vector.reshape(-1, HEAD), first, heads)
+    readout = lax.dynamic_slice_in_dim(payoff_readout_vector.reshape(-1, HEAD), first, heads)
 
     shape = (blocks, heads * group + EXTRA, HEAD)
     pieces = pl.pallas_call(
@@ -140,40 +161,25 @@
         in_specs=[vmem()],
         out_specs=vmem(),
     )(y)
-    pieces = lax.all_to_all(pieces, "ctx", split_axis=0, concat_axis=0, tiled=True)
+    pieces = exchanged(pieces)
     squares = jnp.sum(pieces[:, heads * group : heads * group + 3, :].astype(jnp.float32), axis=1)
     squares = lax.psum(squares, "tp")
 
-    def mine(*tail):
-        return pl.BlockSpec((heads, *tail), lambda g, w: (w[0], *(0 for _ in tail)))
-
-    def whole(*shape):
-        return pl.BlockSpec(shape, lambda g, w: (0,) * len(shape))
-
-    weights = mine(HEAD, HEAD // 2)
     out = pl.pallas_call(
         heads_kernel,
         out_shape=jax.ShapeDtypeStruct(shape, jnp.bfloat16),
-        grid_spec=pltpu.PrefetchScalarGridSpec(
-            num_scalar_prefetch=1,
-            grid=(1,),
-            in_specs=[
-                whole(*shape),
-                whole(*squares.shape),
-                mine(1, HEAD),
-                weights,
-                weights,
-                mine(1, HEAD),
-            ],
-            out_specs=whole(*shape),
-        ),
+        in_specs=[pl.BlockSpec(memory_space=pltpu.SMEM)] + [vmem()] * 5,
+        out_specs=vmem(),
         compiler_params=pltpu.CompilerParams(vmem_limit_bytes=32 * 1024 * 1024),
-    )(where, pieces, squares, gain, probe, lookup, readout)
-    out = lax.all_to_all(out, "ctx", split_axis=0, concat_axis=0, tiled=True)
+    )(usable_extents, pieces, squares, gain, lifting, readout)
+    out = exchanged(out)
     sums = jnp.sum(out[:, heads * group, :].astype(jnp.float32), axis=0)
     handed = lax.ppermute(out, "pipe", [(p, (p + 1) % sections) for p in range(sections)])
-    handed = handed[:, : heads * group].reshape(blocks, heads, group, HEAD)
-    handed = handed.transpose(2, 0, 1, 3).reshape(group, width)
+    tiles = handed[:, : heads * group]
+    tiles = tiles.reshape(SPLIT // 2, blocks // SPLIT, 2, heads, group // 8, 8, HEAD)
+    tiles = tiles.transpose(4, 1, 2, 0, 3, 5, 6).reshape(group // 8, blocks * heads, 8, HEAD)
+    tiles = lax.optimization_barrier(tiles)
+    handed = tiles.transpose(0, 2, 1, 3).reshape(group, width)
     sums = lax.psum(sums, "tp")
     found = jnp.sum(sums[:3]) * lax.rsqrt(jnp.sum(sums[3:6]) / EMBED_DIMENSION + eps_norm)
     return (handed[None, None], found[None, None])

time: 122 us -> 119 us (0.975)
  the two profiles are of different devices: /device:TPU:32 before, /device:TPU:64 now
where the time goes in v3:
time: 119 us; the launch traced here: 118 us
  blocking collectives  46.2 us (39%)
  waiting for transfers between devices  42 us (35%)
  starting transfers between devices  19.5 us (16%)
  Pallas kernels  4.47 us (4%)
  between operations  3.82 us (3%)
  local copies, waits for them, and re-layouts  1.74 us (1%)
    all_to_all x1, blocking collectives, exchanged(): lax.all_to_all(pieces, 'ctx', split_axis=0, concat_axis=0, axis_index_gro...  41.2 us
    all_to_all x1, waiting for transfers between devices, exchanged(): lax.all_to_all(pieces, 'ctx', split_axis=0, concat_axis=0, axis_index_gro...  32.8 us
    all_to_all x1, starting transfers between devices, exchanged(): lax.all_to_all(pieces, 'ctx', split_axis=0, concat_axis=0, axis_index_gro...  16 us
    ppermute x1, waiting for transfers between devices, body(): lax.ppermute(out, 'pipe', [(p, (p + 1) % sections) for p in range(section...  9.16 us
    ppermute x1, starting transfers between devices, body(): lax.ppermute(out, 'pipe', [(p, (p + 1) % sections) for p in range(section...  3.47 us
    psum x1, blocking collectives, body(): squares = lax.psum(squares, 'tp')  2.5 us
    psum x1, blocking collectives, body(): sums = lax.psum(sums, 'tp')  2.46 us
  transfers between devices with their start and end apart: 2, of which 2 were waited for; matrix products, arithmetic and copies ran while one was open for 1% of the time, Pallas kernels for 0%

profile of v3, /device:TPU:64, one launch (start us, length us, event | category | flops | bytes accessed | tf_op | source)
XLA Modules:
  0.0 118.5 jit_solution(15701987338180769420)
XLA Ops:
  0.6 2.1 %shard_map.77 = bf16[16,136,128]{2,1,0:T(8,128)(2,1)} custom-call(bf16[64,4096]{1,0:T(8,128)(2,1)} %bitcast.18), custom_call_target="tpu_custom_call" | custom-call | tf_op jit(solution)/shard_map/pallas_call | solution.py:158
  2.7 0.0 copy-start
  2.7 0.0 copy-start.1
  2.7 16.0 %all-to-all-start = ((bf16[16,136,128]{2,1,0:T(8,128)(2,1)}), bf16[16,136,128]{2,1,0:T(8,128)(2,1)S(1)}, u32[]{:S(2)}, u32[]{:S(2)}) async-start(bf16[16,136,128]{2,1,0:T(8,128)(2,1)} %shard_map.77), calls=%async_computation | async-start | bytes 1114112 | tf_op jit(solution)/shard_map/all_to_all | solution.py:124
  18.7 0.0 copy-start.2
  19.4 0.0 copy-done.2
  19.5 0.1 reduce.1
  19.5 0.7 constant_dynamic-slice_fusion
  20.2 0.0 copy-done
  20.2 0.0 copy-done.1
  20.2 32.8 %all-to-all-done.y_ref = bf16[16,136,128]{2,1,0:T(8,128)(2,1)S(1)} async-done(((bf16[16,136,128]{2,1,0:T(8,128)(2,1)}), bf16[16,136,128]{2,1,0:T(8,128)(2,1)S(1)}, u32[]{:S(2)}, u32[]{:S(2)}) %all-to-all-start) | async-done | bytes 557088 | tf_op jit(solution)/shard_map/all_to_all | solution.py:124
  53.1 2.5 %psum.14.squares_ref = f32[16,128]{1,0:T(8,128)S(1)} all-reduce(f32[16,128]{1,0:T(8,128)S(1)} %convert_reduce_fusion), channel_id=1, replica_groups=mesh['pipe'=16,'ctx'=16,'tp'=2] {'tp'}, use_global_device_ids=true, to_apply=%region_1.0 | all-reduce | flops 2048 | bytes 16384 | tf_op jit(solution)/shard_map/psum | solution.py:166
  55.6 2.4 %shard_map.78 = bf16[16,136,128]{2,1,0:T(8,128)(2,1)S(1)} custom-call(s32[1,1]{1,0:T(1,128)S(6)} %copy.9.length_ref, bf16[16,136,128]{2,1,0:T(8,128)(2,1)S(1)} %all-to-all-done.y_ref, f32[16,128]{1,0:T(8,128)S(1)} %psum.14.squares_ref, bf16[2,128]{1,0:T(2,128)(2,1)S(1)} %get-tuple-element.5.gain_ref, bf16[2,128,128]{2,1,0:T(8,128)(2,1)S(1)} %fusion.lifting_ref, ...), custom_call_target="tpu_custom_call" | custom-call | tf_op jit(solution)/shard_map/pallas_call | solution.py:168
  57.9 41.2 %all_to_all.10 = bf16[16,136,128]{2,1,0:T(8,128)(2,1)S(1)} all-to-all(bf16[16,136,128]{2,1,0:T(8,128)(2,1)S(1)} %shard_map.78), channel_id=1, replica_groups={{0,4,8,12,16,20,24,28,2,6,10,14,18,22,26,30},{1,5,9,13,17,21,25,29,3,7,..., dimensions={0} | all-to-all | bytes 1114112 | tf_op jit(solution)/shard_map/all_to_all | solution.py:124
  99.2 3.5 %collective-permute-start = (bf16[16,136,128]{2,1,0:T(8,128)(2,1)S(1)}, bf16[16,136,128]{2,1,0:T(8,128)(2,1)S(1)}, u32[]{:S(2)}, u32[]{:S(2)}) collective-permute-start(bf16[16,136,128]{2,1,0:T(8,128)(2,1)S(1)} %all_to_all.10), channel_id=1, source_target_pairs={{0,32},{32,64},{64,96},{96,128},{128,160},{160,192},{192,224},{224... | collective-permute-start | bytes 1671176 | tf_op jit(solution)/shard_map/ppermute | solution.py:177
  102.7 2.5 %psum.15 = f32[128]{0:T(128)S(1)} all-reduce(f32[128]{0:T(128)S(1)} %fusion.1), channel_id=1, replica_groups=mesh['pipe'=16,'ctx'=16,'tp'=2] {'tp'}, use_global_device_ids=true, to_apply=%region_3.0 | all-reduce | flops 128 | bytes 1024 | tf_op jit(solution)/shard_map/psum | solution.py:183
  105.2 0.7 slice_reduce_fusion
  107.2 9.2 %collective-permute-done = bf16[16,136,128]{2,1,0:T(8,128)(2,1)S(1)} collective-permute-done((bf16[16,136,128]{2,1,0:T(8,128)(2,1)S(1)}, bf16[16,136,128]{2,1,0:T(8,128)(2,1)S(1)}, u32[]{:S(2)}, u32[]{:S(2)}) %collective-permute-start) | collective-permute-done | bytes 557088 | tf_op jit(solution)/shard_map/ppermute | solution.py:177
  116.4 0.9 copy.8
  (4 shorter events, 0.1 us)
Async XLA Ops:
  2.7 17.5 %copy-start = (bf16[1,1,32,128,64]{3,4,2,1,0:T(8,128)(2,1)S(1)}, bf16[1,1,32,128,64]{3,4,2,1,0:T(8,128)(2,1)}, u32[]{:S(2)}) copy-start(bf16[1,1,32,128,64]{3,4,2,1,0:T(8,128)(2,1)} %param.8) | copy-start | bytes 1572868
  2.7 17.5 %copy-start.1 = (bf16[1,1,32,128,64]{3,4,2,1,0:T(8,128)(2,1)S(1)}, bf16[1,1,32,128,64]{3,4,2,1,0:T(8,128)(2,1)}, u32[]{:S(2)}) copy-start(bf16[1,1,32,128,64]{3,4,2,1,0:T(8,128)(2,1)} %param.9) | copy-start | bytes 1572868
  2.7 50.3 %all-to-all-start = ((bf16[16,136,128]{2,1,0:T(8,128)(2,1)}), bf16[16,136,128]{2,1,0:T(8,128)(2,1)S(1)}, u32[]{:S(2)}, u32[]{:S(2)}) async-start(bf16[16,136,128]{2,1,0:T(8,128)(2,1)} %shard_map.77), calls=%async_computation | async-start | bytes 1114112 | tf_op jit(solution)/shard_map/all_to_all | solution.py:124
  18.7 0.7 copy-start.2
  99.2 17.2 %collective-permute-start = (bf16[16,136,128]{2,1,0:T(8,128)(2,1)S(1)}, bf16[16,136,128]{2,1,0:T(8,128)(2,1)S(1)}, u32[]{:S(2)}, u32[]{:S(2)}) collective-permute-start(bf16[16,136,128]{2,1,0:T(8,128)(2,1)S(1)} %all_to_all.10), channel_id=1, source_target_pairs={{0,32},{32,64},{64,96},{96,128},{128,160},{160,192},{192,224},{224... | collective-permute-start | bytes 1671176 | tf_op jit(solution)/shard_map/ppermute | solution.py:177

commit v4 on v3

--- a/solution.py
+++ b/solution.py
@@ -8,6 +8,7 @@
 EMBED_DIMENSION = 8192
 HEAD = 128
 SPLIT = 4
+TURNS = (((0, 0), (0, 0)), ((0, 0), (0, 0)), ((0, 2), (1, 0)), ((0, 2), (1, 0)))
 EXTRA = 8
 
 eps_norm = 1e-05
@@ -58,8 +59,9 @@
 
 
 def heads_kernel(
-    length_ref, y_ref, squares_ref, gain_ref, lifting_ref, readout_ref, out_ref
+    length_ref, y_ref, squares_ref, gain_ref, lifting_ref, readout_ref, *refs
 ):
+    out_ref = refs[-1]
     length = length_ref[0, 0]
     blocks, heads = y_ref.shape[0], lifting_ref.shape[0]
     group = (y_ref.shape[1] - EXTRA) // heads
@@ -161,6 +163,20 @@
         in_specs=[vmem()],
         out_specs=vmem(),
     )(y)
+    lines, size = blocks // SPLIT, sections // len(TURNS)
+    turn, turns = usable_extents, []
+    for heard in zip(*TURNS):
+        route = [
+            (p * blocks + x * SPLIT + z, p * blocks + (x + dx) % lines * SPLIT + (z + dz) % SPLIT)
+            for p in range(sections)
+            for x in range(lines)
+            for z in range(SPLIT)
+            for dx, dz in [heard[p // size]]
+            if dx or dz
+        ]
+        turn = lax.ppermute(turn, ("pipe", "ctx"), route)
+        turns.append(turn)
+    pieces, *turns = lax.optimization_barrier((pieces, *turns))
     pieces = exchanged(pieces)
     squares = jnp.sum(pieces[:, heads * group : heads * group + 3, :].astype(jnp.float32), axis=1)
     squares = lax.psum(squares, "tp")
@@ -168,10 +184,12 @@
     out = pl.pallas_call(
         heads_kernel,
         out_shape=jax.ShapeDtypeStruct(shape, jnp.bfloat16),
-        in_specs=[pl.BlockSpec(memory_space=pltpu.SMEM)] + [vmem()] * 5,
+        in_specs=[pl.BlockSpec(memory_space=pltpu.SMEM)]
+        + [vmem()] * 5
+        + [pl.BlockSpec(memory_space=pl.ANY)] * len(turns),
         out_specs=vmem(),
         compiler_params=pltpu.CompilerParams(vmem_limit_bytes=32 * 1024 * 1024),
-    )(usable_extents, pieces, squares, gain, lifting, readout)
+    )(usable_extents, pieces, squares, gain, lifting, readout, *turns)
     out = exchanged(out)
     sums = jnp.sum(out[:, heads * group, :].astype(jnp.float32), axis=0)
     handed = lax.ppermute(out, "pipe", [(p, (p + 1) % sections) for p in range(sections)])

time: 119 us -> 112 us (0.941)
  the two profiles are of different devices: /device:TPU:64 before, /device:TPU:1 now
where the time goes in v4:
time: 112 us
  waiting for transfers between devices  40.5 us (36%)
  blocking collectives  35 us (31%)
  starting transfers between devices  24 us (21%)
  Pallas kernels  5.69 us (5%)
  between operations  3.82 us (3%)
  local copies, waits for them, and re-layouts  1.74 us (2%)
    all_to_all x1, blocking collectives, exchanged(): lax.all_to_all(pieces, 'ctx', split_axis=0, concat_axis=0, axis_index_gro...  28.1 us
    all_to_all x1, waiting for transfers between devices, exchanged(): lax.all_to_all(pieces, 'ctx', split_axis=0, concat_axis=0, axis_index_gro...  21.4 us
    ppermute x1, waiting for transfers between devices, body(): lax.ppermute(out, 'pipe', [(p, (p + 1) % sections) for p in range(section...  19.1 us
    all_to_all x1, starting transfers between devices, exchanged(): lax.all_to_all(pieces, 'ctx', split_axis=0, concat_axis=0, axis_index_gro...  18.2 us
    psum x1, blocking collectives, body(): sums = lax.psum(sums, 'tp')  4.2 us
    pallas_call x1, Pallas kernels, body(): pl.pallas_call(heads_kernel, out_shape=jax.ShapeDtypeStruct(shape, jnp.bf...  3.58 us
    ppermute x1, starting transfers between devices, body(): lax.ppermute(out, 'pipe', [(p, (p + 1) % sections) for p in range(section...  3.21 us
    psum x1, blocking collectives, body(): squares = lax.psum(squares, 'tp')  2.7 us
  transfers between devices with their start and end apart: 4, of which 2 were waited for; matrix products, arithmetic and copies ran while one was open for 1% of the time, Pallas kernels for 2%

profile of v4, /device:TPU:1, one launch (start us, length us, event | category | flops | bytes accessed | tf_op | source)
XLA Modules:
  0.0 111.6 jit_solution(5591911195432289799)
XLA Ops:
  0.6 1.2 %collective-permute-start = (s32[1,1]{1,0:T(1,128)}, s32[1,1]{1,0:T(1,128)}, u32[]{:S(2)}, u32[]{:S(2)}) collective-permute-start(s32[1,1]{1,0:T(1,128)} %param.10), channel_id=1, source_target_pairs={{256,260},{258,262},{260,256},{262,258},{264,268},{266,270},{268,2... | collective-permute-start | bytes 20 | tf_op jit(solution)/shard_map/ppermute | solution.py:177
  1.9 2.1 %shard_map.77 = bf16[16,136,128]{2,1,0:T(8,128)(2,1)} custom-call(bf16[64,4096]{1,0:T(8,128)(2,1)} %bitcast.18), custom_call_target="tpu_custom_call" | custom-call | tf_op jit(solution)/shard_map/pallas_call | solution.py:160
  4.0 0.0 copy-start
  4.0 0.0 copy-start.1
  4.0 0.0 collective-permute-done.refs_0_
  4.0 1.3 %collective-permute-start.1 = (s32[1,1]{1,0:T(1,128)}, s32[1,1]{1,0:T(1,128)}, u32[]{:S(2)}, u32[]{:S(2)}) collective-permute-start(s32[1,1]{1,0:T(1,128)} %collective-permute-done.refs_0_), channel_id=1, source_target_pairs={{256,264},{258,266},{260,268},{262,270},{264,272},{266,274},{268,2... | collective-permute-start | bytes 20 | tf_op jit(solution)/shard_map/ppermute | solution.py:177
  5.3 0.0 collective-permute-done.1.refs_1_
  5.3 18.2 %all-to-all-start = ((bf16[16,136,128]{2,1,0:T(8,128)(2,1)}), bf16[16,136,128]{2,1,0:T(8,128)(2,1)S(1)}, u32[]{:S(2)}, u32[]{:S(2)}) async-start(bf16[16,136,128]{2,1,0:T(8,128)(2,1)} %shard_map.77), calls=%async_computation | async-start | bytes 1114112 | tf_op jit(solution)/shard_map/all_to_all | solution.py:126
  23.5 0.0 copy-start.2
  24.2 0.0 copy-done.2
  24.3 0.1 reduce.1
  24.3 0.7 constant_dynamic-slice_fusion
  25.0 0.0 copy-done
  25.0 0.0 copy-done.1
  25.0 21.4 %all-to-all-done.y_ref = bf16[16,136,128]{2,1,0:T(8,128)(2,1)S(1)} async-done(((bf16[16,136,128]{2,1,0:T(8,128)(2,1)}), bf16[16,136,128]{2,1,0:T(8,128)(2,1)S(1)}, u32[]{:S(2)}, u32[]{:S(2)}) %all-to-all-start) | async-done | bytes 557088 | tf_op jit(solution)/shard_map/all_to_all | solution.py:126
  46.5 2.7 %psum.14.squares_ref = f32[16,128]{1,0:T(8,128)S(1)} all-reduce(f32[16,128]{1,0:T(8,128)S(1)} %convert_reduce_fusion), channel_id=1, replica_groups=mesh['pipe'=16,'ctx'=16,'tp'=2] {'tp'}, use_global_device_ids=true, to_apply=%region_1.0 | all-reduce | flops 2048 | bytes 16384 | tf_op jit(solution)/shard_map/psum | solution.py:182
  49.2 3.6 %shard_map.78 = bf16[16,136,128]{2,1,0:T(8,128)(2,1)S(1)} custom-call(s32[1,1]{1,0:T(1,128)S(6)} %copy.9.length_ref, bf16[16,136,128]{2,1,0:T(8,128)(2,1)S(1)} %all-to-all-done.y_ref, f32[16,128]{1,0:T(8,128)S(1)} %psum.14.squares_ref, bf16[2,128]{1,0:T(2,128)(2,1)S(1)} %get-tuple-element.11.gain_ref, bf16[2,128,128]{2,1,0:T(8,128)(2,1)S(1)} %fusion.lifting_ref, ...), custom_call_target="tpu_custom_call" | custom-call | tf_op jit(solution)/shard_map/pallas_call | solution.py:184
  52.8 28.1 %all_to_all.10 = bf16[16,136,128]{2,1,0:T(8,128)(2,1)S(1)} all-to-all(bf16[16,136,128]{2,1,0:T(8,128)(2,1)S(1)} %shard_map.78), channel_id=1, replica_groups={{0,4,8,12,16,20,24,28,2,6,10,14,18,22,26,30},{1,5,9,13,17,21,25,29,3,7,..., dimensions={0} | all-to-all | bytes 1114112 | tf_op jit(solution)/shard_map/all_to_all | solution.py:126
  80.9 3.2 %collective-permute-start.2 = (bf16[16,136,128]{2,1,0:T(8,128)(2,1)S(1)}, bf16[16,136,128]{2,1,0:T(8,128)(2,1)S(1)}, u32[]{:S(2)}, u32[]{:S(2)}) collective-permute-start(bf16[16,136,128]{2,1,0:T(8,128)(2,1)S(1)} %all_to_all.10), channel_id=1, source_target_pairs={{0,32},{32,64},{64,96},{96,128},{128,160},{160,192},{192,224},{224... | collective-permute-start | bytes 1671176 | tf_op jit(solution)/shard_map/ppermute | solution.py:195
  84.1 4.2 %psum.15 = f32[128]{0:T(128)S(1)} all-reduce(f32[128]{0:T(128)S(1)} %fusion.1), channel_id=1, replica_groups=mesh['pipe'=16,'ctx'=16,'tp'=2] {'tp'}, use_global_device_ids=true, to_apply=%region_3.0 | all-reduce | flops 128 | bytes 1024 | tf_op jit(solution)/shard_map/psum | solution.py:201
  88.3 0.7 slice_reduce_fusion
  90.4 19.1 %collective-permute-done.2 = bf16[16,136,128]{2,1,0:T(8,128)(2,1)S(1)} collective-permute-done((bf16[16,136,128]{2,1,0:T(8,128)(2,1)S(1)}, bf16[16,136,128]{2,1,0:T(8,128)(2,1)S(1)}, u32[]{:S(2)}, u32[]{:S(2)}) %collective-permute-start.2) | collective-permute-done | bytes 557088 | tf_op jit(solution)/shard_map/ppermute | solution.py:195
  109.5 0.9 copy.8
  (4 shorter events, 0.1 us)
Async XLA Ops:
  0.6 3.4 %collective-permute-start = (s32[1,1]{1,0:T(1,128)}, s32[1,1]{1,0:T(1,128)}, u32[]{:S(2)}, u32[]{:S(2)}) collective-permute-start(s32[1,1]{1,0:T(1,128)} %param.10), channel_id=1, source_target_pairs={{256,260},{258,262},{260,256},{262,258},{264,268},{266,270},{268,2... | collective-permute-start | bytes 20 | tf_op jit(solution)/shard_map/ppermute | solution.py:177
  4.0 21.0 %copy-start = (bf16[1,1,32,128,64]{3,4,2,1,0:T(8,128)(2,1)S(1)}, bf16[1,1,32,128,64]{3,4,2,1,0:T(8,128)(2,1)}, u32[]{:S(2)}) copy-start(bf16[1,1,32,128,64]{3,4,2,1,0:T(8,128)(2,1)} %param.8) | copy-start | bytes 1572868
  4.0 21.0 %copy-start.1 = (bf16[1,1,32,128,64]{3,4,2,1,0:T(8,128)(2,1)S(1)}, bf16[1,1,32,128,64]{3,4,2,1,0:T(8,128)(2,1)}, u32[]{:S(2)}) copy-start(bf16[1,1,32,128,64]{3,4,2,1,0:T(8,128)(2,1)} %param.9) | copy-start | bytes 1572868
  4.0 1.3 %collective-permute-start.1 = (s32[1,1]{1,0:T(1,128)}, s32[1,1]{1,0:T(1,128)}, u32[]{:S(2)}, u32[]{:S(2)}) collective-permute-start(s32[1,1]{1,0:T(1,128)} %collective-permute-done.refs_0_), channel_id=1, source_target_pairs={{256,264},{258,266},{260,268},{262,270},{264,272},{266,274},{268,2... | collective-permute-start | bytes 20 | tf_op jit(solution)/shard_map/ppermute | solution.py:177
  5.3 41.1 %all-to-all-start = ((bf16[16,136,128]{2,1,0:T(8,128)(2,1)}), bf16[16,136,128]{2,1,0:T(8,128)(2,1)S(1)}, u32[]{:S(2)}, u32[]{:S(2)}) async-start(bf16[16,136,128]{2,1,0:T(8,128)(2,1)} %shard_map.77), calls=%async_computation | async-start | bytes 1114112 | tf_op jit(solution)/shard_map/all_to_all | solution.py:126
  23.5 0.7 copy-start.2
  80.9 28.6 %collective-permute-start.2 = (bf16[16,136,128]{2,1,0:T(8,128)(2,1)S(1)}, bf16[16,136,128]{2,1,0:T(8,128)(2,1)S(1)}, u32[]{:S(2)}, u32[]{:S(2)}) collective-permute-start(bf16[16,136,128]{2,1,0:T(8,128)(2,1)S(1)} %all_to_all.10), channel_id=1, source_target_pairs={{0,32},{32,64},{64,96},{96,128},{128,160},{160,192},{192,224},{224... | collective-permute-start | bytes 1671176 | tf_op jit(solution)/shard_map/ppermute | solution.py:195

commit v5 on v3

--- a/solution.py
+++ b/solution.py
@@ -8,6 +8,7 @@
 EMBED_DIMENSION = 8192
 HEAD = 128
 SPLIT = 4
+TURNS = ((2, 2, 2),)
 EXTRA = 8
 
 eps_norm = 1e-05
@@ -26,19 +27,22 @@
     return parts
 
 
-def cut_kernel(y_ref, pieces_ref):
+def squares_kernel(y_ref, out_ref):
+    total = jnp.zeros((y_ref.shape[0], HEAD), jnp.float32)
+    for j in range(0, y_ref.shape[1], HEAD):
+        part = y_ref[:, j : j + HEAD].astype(jnp.float32)
+        total = total + part * part
+    out_ref[...] = jnp.sum(total.T, axis=0, keepdims=True)
+
+
+def cut_kernel(y_ref, squares_ref, pieces_ref):
     blocks, group = pieces_ref.shape[0], y_ref.shape[0]
     heads = y_ref.shape[1] // HEAD // blocks
-    total = jnp.zeros((group, HEAD), jnp.float32)
     for n, j in enumerate(ordered(blocks)):
         for h in range(heads):
             cols = slice((j * heads + h) * HEAD, (j * heads + h + 1) * HEAD)
-            part = y_ref[:, cols]
-            pieces_ref[n, h * group : (h + 1) * group, :] = part
-            part = part.astype(jnp.float32)
-            total = total + part * part
-    total = jnp.concatenate([total, jnp.zeros((HEAD - group, HEAD), jnp.float32)], axis=0)
-    total = jnp.sum(total.T, axis=0, keepdims=True)
+            pieces_ref[n, h * group : (h + 1) * group, :] = y_ref[:, cols]
+    total = jnp.concatenate([squares_ref[...], jnp.zeros((1, HEAD - group), jnp.float32)], axis=1)
     rows = three(total) + [jnp.zeros((EXTRA - 3, HEAD), jnp.float32)]
     rows = jnp.concatenate(rows, axis=0).astype(jnp.bfloat16)
     for j in range(blocks):
@@ -58,9 +62,10 @@
 
 
 def heads_kernel(
-    length_ref, y_ref, squares_ref, gain_ref, lifting_ref, readout_ref, out_ref
+    length_ref, y_ref, gain_ref, lifting_ref, readout_ref, *refs
 ):
-    length = length_ref[0, 0]
+    out_ref = refs[-1]
+    length, behind = length_ref[0, 0], length_ref[0, 1]
     blocks, heads = y_ref.shape[0], lifting_ref.shape[0]
     group = (y_ref.shape[1] - EXTRA) // heads
     lines = blocks // SPLIT
@@ -75,7 +80,8 @@
     place = [order.index(j) for j in range(blocks)]
     scales = []
     for j in range(blocks):
-        row = squares_ref[place[j] : place[j] + 1, :group]
+        row = y_ref[place[j], heads * group :, :].astype(jnp.float32)
+        row = jnp.sum(row, axis=0, keepdims=True)[:, :group]
         scale = lax.rsqrt(row / EMBED_DIMENSION + eps_norm)
         scales.append(jnp.broadcast_to(scale, (HEAD, group)).T)
     product = jnp.zeros((1, 1), jnp.float32)
@@ -105,7 +111,9 @@
             out = out + jnp.concatenate(y[x * SPLIT : (x + 1) * SPLIT], axis=0)
             out = jnp.where(at < length - x * chunk, out, 0.0).astype(jnp.bfloat16)
             for z in range(SPLIT):
-                out_ref[place[x * SPLIT + z], rows, :] = out[z * group : (z + 1) * group]
+                to = lax.rem(z + SPLIT - behind, SPLIT)
+                to = lax.rem(to, SPLIT // 2) * 2 * lines + x * 2 + lax.div(to, SPLIT // 2)
+                out_ref[to, rows, :] = out[z * group : (z + 1) * group]
             out = jnp.where(at == length - 1 - x * chunk, out.astype(jnp.float32), 0.0)
             last = last + jnp.sum(out, axis=0, keepdims=True)
             if x + 1 < lines:
@@ -154,27 +162,66 @@
     gain = lax.dynamic_slice_in_dim(entry_rescale_vector.reshape(-1, HEAD), first, heads)
     readout = lax.dynamic_slice_in_dim(payoff_readout_vector.reshape(-1, HEAD), first, heads)
 
+    squares = pl.pallas_call(
+        squares_kernel,
+        out_shape=jax.ShapeDtypeStruct((1, group), jnp.float32),
+        in_specs=[vmem()],
+        out_specs=vmem(),
+    )(y)
+    squares = lax.psum(squares, "tp")
+    turn, squares = lax.optimization_barrier((usable_extents, squares))
+    lines, runs, sides, turns = blocks // SPLIT, 4, lax.axis_size("tp"), []
+    for dy, dx, dz in TURNS:
+        route = [
+            (
+                ((p * lines + x) * SPLIT + z) * sides + sides - 1,
+                (
+                    ((p // runs * runs + (p + dy) % runs) * lines + (x + dx) % lines) * SPLIT
+                    + (z + dz) % SPLIT
+                )
+                * sides
+                + sides
+                - 1,
+            )
+            for p in range(sections)
+            for x in range(lines)
+            for z in range(SPLIT)
+        ]
+        turn = lax.ppermute(turn, ("pipe", "ctx", "tp"), route)
+        turns.append(turn)
+
     shape = (blocks, heads * group + EXTRA, HEAD)
     pieces = pl.pallas_call(
         cut_kernel,
         out_shape=jax.ShapeDtypeStruct(shape, jnp.bfloat16),
-        in_specs=[vmem()],
+        in_specs=[vmem(), vmem()],
         out_specs=vmem(),
-    )(y)
+    )(y, squares)
+    pieces, *turns = lax.optimization_barrier((pieces, *turns))
     pieces = exchanged(pieces)
-    squares = jnp.sum(pieces[:, heads * group : heads * group + 3, :].astype(jnp.float32), axis=1)
-    squares = lax.psum(squares, "tp")
-
+    behind = (lax.axis_index("pipe") == sections - 1).astype(jnp.int32)
+    extents = jnp.concatenate([usable_extents, behind.reshape(1, 1)], axis=1)
     out = pl.pallas_call(
         heads_kernel,
         out_shape=jax.ShapeDtypeStruct(shape, jnp.bfloat16),
-        in_specs=[pl.BlockSpec(memory_space=pltpu.SMEM)] + [vmem()] * 5,
+        in_specs=[pl.BlockSpec(memory_space=pltpu.SMEM)]
+        + [vmem()] * 4
+        + [pl.BlockSpec(memory_space=pl.ANY)] * len(turns),
         out_specs=vmem(),
         compiler_params=pltpu.CompilerParams(vmem_limit_bytes=32 * 1024 * 1024),
-    )(usable_extents, pieces, squares, gain, lifting, readout)
+    )(extents, pieces, gain, lifting, readout, *turns)
     out = exchanged(out)
     sums = jnp.sum(out[:, heads * group, :].astype(jnp.float32), axis=0)
-    handed = lax.ppermute(out, "pipe", [(p, (p + 1) % sections) for p in range(sections)])
+    route = [
+        (
+            (p * lines + x) * SPLIT + z,
+            ((p + 1) % sections * lines + x) * SPLIT + (z + (p + 1) // sections) % SPLIT,
+        )
+        for p in range(sections)
+        for x in range(lines)
+        for z in range(SPLIT)
+    ]
+    handed = lax.ppermute(out, ("pipe", "ctx"), route)
     tiles = handed[:, : heads * group]
     tiles = tiles.reshape(SPLIT // 2, blocks // SPLIT, 2, heads, group // 8, 8, HEAD)
     tiles = tiles.transpose(4, 1, 2, 0, 3, 5, 6).reshape(group // 8, blocks * heads, 8, HEAD)

time: 119 us -> 111 us (0.933)
  the two profiles are of different devices: /device:TPU:64 before, /device:TPU:1 now
where the time goes in v5:
time: 111 us
  blocking collectives  39.8 us (36%)
  starting transfers between devices  30.4 us (27%)
  waiting for transfers between devices  26.8 us (24%)
  Pallas kernels  7.22 us (7%)
  between operations  3.83 us (3%)
  local copies, waits for them, and re-layouts  1.73 us (2%)
    all_to_all x1, blocking collectives, exchanged(): lax.all_to_all(pieces, 'ctx', split_axis=0, concat_axis=0, axis_index_gro...  27.8 us
    all_to_all x1, waiting for transfers between devices, exchanged(): lax.all_to_all(pieces, 'ctx', split_axis=0, concat_axis=0, axis_index_gro...  19.6 us
    ppermute x1, starting transfers between devices, body(): turn = lax.ppermute(turn, ('pipe', 'ctx', 'tp'), route)  15.2 us
    all_to_all x1, starting transfers between devices, exchanged(): lax.all_to_all(pieces, 'ctx', split_axis=0, concat_axis=0, axis_index_gro...  12 us
    psum x1, blocking collectives, body(): squares = lax.psum(squares, 'tp')  9.61 us
    ppermute x1, waiting for transfers between devices, body(): handed = lax.ppermute(out, ('pipe', 'ctx'), route)  6.2 us
    pallas_call x1, Pallas kernels, body(): pl.pallas_call(heads_kernel, out_shape=jax.ShapeDtypeStruct(shape, jnp.bf...  3.53 us
    ppermute x1, starting transfers between devices, body(): handed = lax.ppermute(out, ('pipe', 'ctx'), route)  3.25 us
  transfers between devices with their start and end apart: 3, of which 3 were waited for; matrix products, arithmetic and copies ran while one was open for 1% of the time, Pallas kernels for 2%

profile of v5, /device:TPU:1, one launch (start us, length us, event | category | flops | bytes accessed | tf_op | source)
XLA Modules:
  0.0 110.6 jit_solution(8270525930456940013)
XLA Ops:
  0.6 1.8 %shard_map.77 = f32[1,64]{1,0:T(1,128)} custom-call(bf16[64,4096]{1,0:T(8,128)(2,1)} %bitcast.18), custom_call_target="tpu_custom_call" | custom-call | tf_op jit(solution)/shard_map/pallas_call | solution.py:165
  2.4 9.6 %psum.14.squares_ref = f32[1,64]{1,0:T(1,128)} all-reduce(f32[1,64]{1,0:T(1,128)} %shard_map.77), channel_id=1, replica_groups=mesh['pipe'=16,'ctx'=16,'tp'=2] {'tp'}, use_global_device_ids=true, to_apply=%region_0.0 | all-reduce | flops 64 | bytes 512 | tf_op jit(solution)/shard_map/psum | solution.py:171
  12.0 15.2 %collective-permute-start = (s32[1,1]{1,0:T(1,128)}, s32[1,1]{1,0:T(1,128)}, u32[]{:S(2)}, u32[]{:S(2)}) collective-permute-start(s32[1,1]{1,0:T(1,128)} %param.10), channel_id=1, source_target_pairs={{1,85},{3,87},{5,81},{7,83},{9,93},{11,95},{13,89},{15,91},{17,69}... | collective-permute-start | bytes 20 | tf_op jit(solution)/shard_map/ppermute | solution.py:190
  27.2 1.9 %shard_map.78 = bf16[16,136,128]{2,1,0:T(8,128)(2,1)} custom-call(bf16[64,4096]{1,0:T(8,128)(2,1)} %bitcast.19, f32[1,64]{1,0:T(1,128)} %psum.14.squares_ref), custom_call_target="tpu_custom_call" | custom-call | tf_op jit(solution)/shard_map/pallas_call | solution.py:194
  29.1 0.0 copy-start
  29.1 0.0 copy-start.1
  29.1 0.9 collective-permute-done.refs_0_
  30.0 12.0 %all-to-all-start = ((bf16[16,136,128]{2,1,0:T(8,128)(2,1)}), bf16[16,136,128]{2,1,0:T(8,128)(2,1)S(1)}, u32[]{:S(2)}, u32[]{:S(2)}) async-start(bf16[16,136,128]{2,1,0:T(8,128)(2,1)} %shard_map.78), calls=%async_computation | async-start | bytes 1114112 | tf_op jit(solution)/shard_map/all_to_all | solution.py:132
  42.0 0.0 copy-start.2
  42.7 0.0 copy-done.2
  42.8 0.1 reduce.1
  42.8 0.1 pad_add_fusion.length_ref
  42.9 0.7 constant_dynamic-slice_fusion
  43.6 0.0 copy-done
  43.6 0.0 copy-done.1
  43.6 19.6 %all-to-all-done.y_ref = bf16[16,136,128]{2,1,0:T(8,128)(2,1)S(1)} async-done(((bf16[16,136,128]{2,1,0:T(8,128)(2,1)}), bf16[16,136,128]{2,1,0:T(8,128)(2,1)S(1)}, u32[]{:S(2)}, u32[]{:S(2)}) %all-to-all-start) | async-done | bytes 557088 | tf_op jit(solution)/shard_map/all_to_all | solution.py:132
  63.2 3.5 %shard_map.79 = bf16[16,136,128]{2,1,0:T(8,128)(2,1)S(1)} custom-call(s32[1,2]{1,0:T(1,128)S(1)} %pad_add_fusion.length_ref, bf16[16,136,128]{2,1,0:T(8,128)(2,1)S(1)} %all-to-all-done.y_ref, bf16[2,128]{1,0:T(2,128)(2,1)S(1)} %get-tuple-element.13.gain_ref, bf16[2,128,128]{2,1,0:T(8,128)(2,1)S(1)} %fusion.lifting_ref, ...), custom_call_target="tpu_custom_call" | custom-call | tf_op jit(solution)/shard_map/pallas_call | solution.py:204
  66.8 27.8 %all_to_all.10 = bf16[16,136,128]{2,1,0:T(8,128)(2,1)S(1)} all-to-all(bf16[16,136,128]{2,1,0:T(8,128)(2,1)S(1)} %shard_map.79), channel_id=1, replica_groups={{0,4,8,12,16,20,24,28,2,6,10,14,18,22,26,30},{1,5,9,13,17,21,25,29,3,7,..., dimensions={0} | all-to-all | bytes 1114112 | tf_op jit(solution)/shard_map/all_to_all | solution.py:132
  94.5 3.2 %collective-permute-start.1 = (bf16[16,136,128]{2,1,0:T(8,128)(2,1)S(1)}, bf16[16,136,128]{2,1,0:T(8,128)(2,1)S(1)}, u32[]{:S(2)}, u32[]{:S(2)}) collective-permute-start(bf16[16,136,128]{2,1,0:T(8,128)(2,1)S(1)} %all_to_all.10), channel_id=1, source_target_pairs={{0,32},{2,34},{4,36},{6,38},{8,40},{10,42},{12,44},{14,46},{16,48}... | collective-permute-start | bytes 1671176 | tf_op jit(solution)/shard_map/ppermute | solution.py:224
  97.8 2.5 %psum.15 = f32[128]{0:T(128)S(1)} all-reduce(f32[128]{0:T(128)S(1)} %fusion.1), channel_id=1, replica_groups=mesh['pipe'=16,'ctx'=16,'tp'=2] {'tp'}, use_global_device_ids=true, to_apply=%region_2.0 | all-reduce | flops 128 | bytes 1024 | tf_op jit(solution)/shard_map/psum | solution.py:230
  100.3 0.7 slice_reduce_fusion
  102.3 6.2 %collective-permute-done.1 = bf16[16,136,128]{2,1,0:T(8,128)(2,1)S(1)} collective-permute-done((bf16[16,136,128]{2,1,0:T(8,128)(2,1)S(1)}, bf16[16,136,128]{2,1,0:T(8,128)(2,1)S(1)}, u32[]{:S(2)}, u32[]{:S(2)}) %collective-permute-start.1) | collective-permute-done | bytes 557088 | tf_op jit(solution)/shard_map/ppermute | solution.py:224
  108.6 0.9 copy.8
  (3 shorter events, 0.1 us)
Async XLA Ops:
  12.0 18.0 %collective-permute-start = (s32[1,1]{1,0:T(1,128)}, s32[1,1]{1,0:T(1,128)}, u32[]{:S(2)}, u32[]{:S(2)}) collective-permute-start(s32[1,1]{1,0:T(1,128)} %param.10), channel_id=1, source_target_pairs={{1,85},{3,87},{5,81},{7,83},{9,93},{11,95},{13,89},{15,91},{17,69}... | collective-permute-start | bytes 20 | tf_op jit(solution)/shard_map/ppermute | solution.py:190
  29.1 14.5 %copy-start = (bf16[1,1,32,128,64]{3,4,2,1,0:T(8,128)(2,1)S(1)}, bf16[1,1,32,128,64]{3,4,2,1,0:T(8,128)(2,1)}, u32[]{:S(2)}) copy-start(bf16[1,1,32,128,64]{3,4,2,1,0:T(8,128)(2,1)} %param.8) | copy-start | bytes 1572868
  29.1 14.5 %copy-start.1 = (bf16[1,1,32,128,64]{3,4,2,1,0:T(8,128)(2,1)S(1)}, bf16[1,1,32,128,64]{3,4,2,1,0:T(8,128)(2,1)}, u32[]{:S(2)}) copy-start(bf16[1,1,32,128,64]{3,4,2,1,0:T(8,128)(2,1)} %param.9) | copy-start | bytes 1572868
  30.0 33.2 %all-to-all-start = ((bf16[16,136,128]{2,1,0:T(8,128)(2,1)}), bf16[16,136,128]{2,1,0:T(8,128)(2,1)S(1)}, u32[]{:S(2)}, u32[]{:S(2)}) async-start(bf16[16,136,128]{2,1,0:T(8,128)(2,1)} %shard_map.78), calls=%async_computation | async-start | bytes 1114112 | tf_op jit(solution)/shard_map/all_to_all | solution.py:132
  42.0 0.7 copy-start.2
  94.5 14.0 %collective-permute-start.1 = (bf16[16,136,128]{2,1,0:T(8,128)(2,1)S(1)}, bf16[16,136,128]{2,1,0:T(8,128)(2,1)S(1)}, u32[]{:S(2)}, u32[]{:S(2)}) collective-permute-start(bf16[16,136,128]{2,1,0:T(8,128)(2,1)S(1)} %all_to_all.10), channel_id=1, source_target_pairs={{0,32},{2,34},{4,36},{6,38},{8,40},{10,42},{12,44},{14,46},{16,48}... | collective-permute-start | bytes 1671176 | tf_op jit(solution)/shard_map/ppermute | solution.py:224

commit v6 on v5

--- a/solution.py
+++ b/solution.py
@@ -62,10 +62,10 @@
 
 
 def heads_kernel(
-    length_ref, y_ref, gain_ref, lifting_ref, readout_ref, *refs
+    length_ref, behind_ref, y_ref, squares_ref, gain_ref, lifting_ref, readout_ref, *refs
 ):
     out_ref = refs[-1]
-    length, behind = length_ref[0, 0], length_ref[0, 1]
+    length, behind = length_ref[0, 0], behind_ref[0, 0]
     blocks, heads = y_ref.shape[0], lifting_ref.shape[0]
     group = (y_ref.shape[1] - EXTRA) // heads
     lines = blocks // SPLIT
@@ -78,10 +78,11 @@
     ones = jnp.ones((chunk, HEAD), jnp.bfloat16)
     order = ordered(blocks)
     place = [order.index(j) for j in range(blocks)]
+    to = [lax.rem(z + SPLIT - behind, SPLIT) for z in range(SPLIT)]
+    to = [lax.rem(z, SPLIT // 2) * 2 * lines + lax.div(z, SPLIT // 2) for z in to]
     scales = []
     for j in range(blocks):
-        row = y_ref[place[j], heads * group :, :].astype(jnp.float32)
-        row = jnp.sum(row, axis=0, keepdims=True)[:, :group]
+        row = squares_ref[place[j] : place[j] + 1, :group]
         scale = lax.rsqrt(row / EMBED_DIMENSION + eps_norm)
         scales.append(jnp.broadcast_to(scale, (HEAD, group)).T)
     product = jnp.zeros((1, 1), jnp.float32)
@@ -111,9 +112,7 @@
             out = out + jnp.concatenate(y[x * SPLIT : (x + 1) * SPLIT], axis=0)
             out = jnp.where(at < length - x * chunk, out, 0.0).astype(jnp.bfloat16)
             for z in range(SPLIT):
-                to = lax.rem(z + SPLIT - behind, SPLIT)
-                to = lax.rem(to, SPLIT // 2) * 2 * lines + x * 2 + lax.div(to, SPLIT // 2)
-                out_ref[to, rows, :] = out[z * group : (z + 1) * group]
+                out_ref[to[z] + x * 2, rows, :] = out[z * group : (z + 1) * group]
             out = jnp.where(at == length - 1 - x * chunk, out.astype(jnp.float32), 0.0)
             last = last + jnp.sum(out, axis=0, keepdims=True)
             if x + 1 < lines:
@@ -169,7 +168,7 @@
         out_specs=vmem(),
     )(y)
     squares = lax.psum(squares, "tp")
-    turn, squares = lax.optimization_barrier((usable_extents, squares))
+    turn = squares
     lines, runs, sides, turns = blocks // SPLIT, 4, lax.axis_size("tp"), []
     for dy, dx, dz in TURNS:
         route = [
@@ -199,17 +198,17 @@
     )(y, squares)
     pieces, *turns = lax.optimization_barrier((pieces, *turns))
     pieces = exchanged(pieces)
+    squares = jnp.sum(pieces[:, heads * group : heads * group + 3, :].astype(jnp.float32), axis=1)
     behind = (lax.axis_index("pipe") == sections - 1).astype(jnp.int32)
-    extents = jnp.concatenate([usable_extents, behind.reshape(1, 1)], axis=1)
     out = pl.pallas_call(
         heads_kernel,
         out_shape=jax.ShapeDtypeStruct(shape, jnp.bfloat16),
-        in_specs=[pl.BlockSpec(memory_space=pltpu.SMEM)]
-        + [vmem()] * 4
+        in_specs=[pl.BlockSpec(memory_space=pltpu.SMEM)] * 2
+        + [vmem()] * 5
         + [pl.BlockSpec(memory_space=pl.ANY)] * len(turns),
         out_specs=vmem(),
         compiler_params=pltpu.CompilerParams(vmem_limit_bytes=32 * 1024 * 1024),
-    )(extents, pieces, gain, lifting, readout, *turns)
+    )(usable_extents, behind.reshape(1, 1), pieces, squares, gain, lifting, readout, *turns)
     out = exchanged(out)
     sums = jnp.sum(out[:, heads * group, :].astype(jnp.float32), axis=0)
     route = [

time: 111 us -> 110 us (level)
  Pallas kernels: 7.22 us -> 6.04 us
    pallas_call x1, Pallas kernels: 3.53 us -> 2.34 us  [body(): pl.pallas_call(heads_kernel, out_shape=jax.ShapeDtypeStruct(shape, jnp.bf...]
where the time goes in v6:
time: 110 us; the launch traced here: 109 us
  blocking collectives  40.1 us (36%)
  starting transfers between devices  30.3 us (28%)
  waiting for transfers between devices  26.3 us (24%)
  Pallas kernels  6.04 us (5%)
  between operations  3.83 us (3%)
  local copies, waits for them, and re-layouts  1.74 us (2%)
    all_to_all x1, blocking collectives, exchanged(): lax.all_to_all(pieces, 'ctx', split_axis=0, concat_axis=0, axis_index_gro...  28.6 us
    all_to_all x1, waiting for transfers between devices, exchanged(): lax.all_to_all(pieces, 'ctx', split_axis=0, concat_axis=0, axis_index_gro...  19.5 us
    ppermute x1, starting transfers between devices, body(): turn = lax.ppermute(turn, ('pipe', 'ctx', 'tp'), route)  15.1 us
    all_to_all x1, starting transfers between devices, exchanged(): lax.all_to_all(pieces, 'ctx', split_axis=0, concat_axis=0, axis_index_gro...  12 us
    psum x1, blocking collectives, body(): squares = lax.psum(squares, 'tp')  9.11 us
    ppermute x1, waiting for transfers between devices, body(): handed = lax.ppermute(out, ('pipe', 'ctx'), route)  6.08 us
    ppermute x1, starting transfers between devices, body(): handed = lax.ppermute(out, ('pipe', 'ctx'), route)  3.17 us
    psum x1, blocking collectives, body(): sums = lax.psum(sums, 'tp')  2.47 us
  transfers between devices with their start and end apart: 3, of which 3 were waited for; matrix products, arithmetic and copies ran while one was open for 1% of the time, Pallas kernels for 2%

profile of v6, /device:TPU:1, one launch (start us, length us, event | category | flops | bytes accessed | tf_op | source)
XLA Modules:
  0.0 109.1 jit_solution(16135881836350054842)
XLA Ops:
  0.6 1.8 %shard_map.77 = f32[1,64]{1,0:T(1,128)} custom-call(bf16[64,4096]{1,0:T(8,128)(2,1)} %bitcast.18), custom_call_target="tpu_custom_call" | custom-call | tf_op jit(solution)/shard_map/pallas_call | solution.py:164
  2.4 9.1 %psum.14.squares_ref = f32[1,64]{1,0:T(1,128)S(1)} all-reduce(f32[1,64]{1,0:T(1,128)} %shard_map.77), channel_id=1, replica_groups=mesh['pipe'=16,'ctx'=16,'tp'=2] {'tp'}, use_global_device_ids=true, to_apply=%region_0.0 | all-reduce | flops 64 | bytes 512 | tf_op jit(solution)/shard_map/psum | solution.py:170
  11.5 0.0 copy-start.3
  11.5 15.1 %collective-permute-start = (f32[1,64]{1,0:T(1,128)S(1)}, f32[1,64]{1,0:T(1,128)S(1)}, u32[]{:S(2)}, u32[]{:S(2)}) collective-permute-start(f32[1,64]{1,0:T(1,128)S(1)} %psum.14.squares_ref), channel_id=1, source_target_pairs={{1,85},{3,87},{5,81},{7,83},{9,93},{11,95},{13,89},{15,91},{17,69}... | collective-permute-start | bytes 776 | tf_op jit(solution)/shard_map/ppermute | solution.py:189
  26.7 0.0 copy-done.3
  26.7 1.9 %shard_map.78 = bf16[16,136,128]{2,1,0:T(8,128)(2,1)} custom-call(bf16[64,4096]{1,0:T(8,128)(2,1)} %bitcast.19, f32[1,64]{1,0:T(1,128)} %copy-done.3), custom_call_target="tpu_custom_call" | custom-call | tf_op jit(solution)/shard_map/pallas_call | solution.py:193
  28.6 0.0 copy-start
  28.6 0.0 copy-start.1
  28.6 0.7 collective-permute-done.refs_0_
  29.3 12.0 %all-to-all-start = ((bf16[16,136,128]{2,1,0:T(8,128)(2,1)}), bf16[16,136,128]{2,1,0:T(8,128)(2,1)S(1)}, u32[]{:S(2)}, u32[]{:S(2)}) async-start(bf16[16,136,128]{2,1,0:T(8,128)(2,1)} %shard_map.78), calls=%async_computation | async-start | bytes 1114112 | tf_op jit(solution)/shard_map/all_to_all | solution.py:131
  41.3 0.0 copy-start.2
  42.0 0.0 copy-done.2
  42.0 0.1 reduce.1
  42.1 0.7 constant_dynamic-slice_fusion
  42.8 0.0 copy-done
  42.8 0.0 copy-done.1
  42.8 19.5 %all-to-all-done.y_ref = bf16[16,136,128]{2,1,0:T(8,128)(2,1)S(1)} async-done(((bf16[16,136,128]{2,1,0:T(8,128)(2,1)}), bf16[16,136,128]{2,1,0:T(8,128)(2,1)S(1)}, u32[]{:S(2)}, u32[]{:S(2)}) %all-to-all-start) | async-done | bytes 557088 | tf_op jit(solution)/shard_map/all_to_all | solution.py:131
  62.3 2.3 %shard_map.79 = bf16[16,136,128]{2,1,0:T(8,128)(2,1)S(1)} custom-call(s32[1,1]{1,0:T(1,128)S(6)} %copy.9.length_ref, s32[1,1]{1,0:T(1,128)} %bitcast.behind_ref, bf16[16,136,128]{2,1,0:T(8,128)(2,1)S(1)} %all-to-all-done.y_ref, f32[16,128]{1,0:T(8,128)S(1)} %convert_reduce_fusion.squares_ref, bf16[2,128]{1,0:T(2,128)(2,1)S(1)} %get-tuple-element.9.gain_ref, ...), custom_call_target="tpu_custom_call" | custom-call | tf_op jit(solution)/shard_map/pallas_call | solution.py:203
  64.7 28.6 %all_to_all.10 = bf16[16,136,128]{2,1,0:T(8,128)(2,1)S(1)} all-to-all(bf16[16,136,128]{2,1,0:T(8,128)(2,1)S(1)} %shard_map.79), channel_id=1, replica_groups={{0,4,8,12,16,20,24,28,2,6,10,14,18,22,26,30},{1,5,9,13,17,21,25,29,3,7,..., dimensions={0} | all-to-all | bytes 1114112 | tf_op jit(solution)/shard_map/all_to_all | solution.py:131
  93.2 3.2 %collective-permute-start.1 = (bf16[16,136,128]{2,1,0:T(8,128)(2,1)S(1)}, bf16[16,136,128]{2,1,0:T(8,128)(2,1)S(1)}, u32[]{:S(2)}, u32[]{:S(2)}) collective-permute-start(bf16[16,136,128]{2,1,0:T(8,128)(2,1)S(1)} %all_to_all.10), channel_id=1, source_target_pairs={{0,32},{2,34},{4,36},{6,38},{8,40},{10,42},{12,44},{14,46},{16,48}... | collective-permute-start | bytes 1671176 | tf_op jit(solution)/shard_map/ppermute | solution.py:223
  96.4 2.5 %psum.15 = f32[128]{0:T(128)S(1)} all-reduce(f32[128]{0:T(128)S(1)} %fusion.1), channel_id=1, replica_groups=mesh['pipe'=16,'ctx'=16,'tp'=2] {'tp'}, use_global_device_ids=true, to_apply=%region_3.0 | all-reduce | flops 128 | bytes 1024 | tf_op jit(solution)/shard_map/psum | solution.py:229
  98.9 0.7 slice_reduce_fusion
  100.9 6.1 %collective-permute-done.1 = bf16[16,136,128]{2,1,0:T(8,128)(2,1)S(1)} collective-permute-done((bf16[16,136,128]{2,1,0:T(8,128)(2,1)S(1)}, bf16[16,136,128]{2,1,0:T(8,128)(2,1)S(1)}, u32[]{:S(2)}, u32[]{:S(2)}) %collective-permute-start.1) | collective-permute-done | bytes 557088 | tf_op jit(solution)/shard_map/ppermute | solution.py:223
  107.1 0.9 copy.8
  (4 shorter events, 0.1 us)
Async XLA Ops:
  11.5 15.2 %copy-start.3 = (f32[1,64]{1,0:T(1,128)}, f32[1,64]{1,0:T(1,128)S(1)}, u32[]{:S(2)}) copy-start(f32[1,64]{1,0:T(1,128)S(1)} %psum.14.squares_ref) | copy-start | bytes 772
  11.5 17.8 %collective-permute-start = (f32[1,64]{1,0:T(1,128)S(1)}, f32[1,64]{1,0:T(1,128)S(1)}, u32[]{:S(2)}, u32[]{:S(2)}) collective-permute-start(f32[1,64]{1,0:T(1,128)S(1)} %psum.14.squares_ref), channel_id=1, source_target_pairs={{1,85},{3,87},{5,81},{7,83},{9,93},{11,95},{13,89},{15,91},{17,69}... | collective-permute-start | bytes 776 | tf_op jit(solution)/shard_map/ppermute | solution.py:189
  28.6 14.2 %copy-start = (bf16[1,1,32,128,64]{3,4,2,1,0:T(8,128)(2,1)S(1)}, bf16[1,1,32,128,64]{3,4,2,1,0:T(8,128)(2,1)}, u32[]{:S(2)}) copy-start(bf16[1,1,32,128,64]{3,4,2,1,0:T(8,128)(2,1)} %param.8) | copy-start | bytes 1572868
  28.6 14.2 %copy-start.1 = (bf16[1,1,32,128,64]{3,4,2,1,0:T(8,128)(2,1)S(1)}, bf16[1,1,32,128,64]{3,4,2,1,0:T(8,128)(2,1)}, u32[]{:S(2)}) copy-start(bf16[1,1,32,128,64]{3,4,2,1,0:T(8,128)(2,1)} %param.9) | copy-start | bytes 1572868
  29.3 33.0 %all-to-all-start = ((bf16[16,136,128]{2,1,0:T(8,128)(2,1)}), bf16[16,136,128]{2,1,0:T(8,128)(2,1)S(1)}, u32[]{:S(2)}, u32[]{:S(2)}) async-start(bf16[16,136,128]{2,1,0:T(8,128)(2,1)} %shard_map.78), calls=%async_computation | async-start | bytes 1114112 | tf_op jit(solution)/shard_map/all_to_all | solution.py:131
  41.3 0.7 copy-start.2
  93.2 13.8 %collective-permute-start.1 = (bf16[16,136,128]{2,1,0:T(8,128)(2,1)S(1)}, bf16[16,136,128]{2,1,0:T(8,128)(2,1)S(1)}, u32[]{:S(2)}, u32[]{:S(2)}) collective-permute-start(bf16[16,136,128]{2,1,0:T(8,128)(2,1)S(1)} %all_to_all.10), channel_id=1, source_target_pairs={{0,32},{2,34},{4,36},{6,38},{8,40},{10,42},{12,44},{14,46},{16,48}... | collective-permute-start | bytes 1671176 | tf_op jit(solution)/shard_map/ppermute | solution.py:223

commit v7 on v6

--- a/solution.py
+++ b/solution.py
@@ -19,6 +19,11 @@
     return [x * SPLIT + z + far * n for z in range(far) for x in range(lines) for n in range(2)]
 
 
+def rotated(blocks):
+    lines = blocks // SPLIT
+    return [x * SPLIT + (z + x) % SPLIT for x in range(lines) for z in range(SPLIT)]
+
+
 def three(value):
     parts = []
     for _ in range(3):
@@ -38,7 +43,7 @@
 def cut_kernel(y_ref, squares_ref, pieces_ref):
     blocks, group = pieces_ref.shape[0], y_ref.shape[0]
     heads = y_ref.shape[1] // HEAD // blocks
-    for n, j in enumerate(ordered(blocks)):
+    for n, j in enumerate(rotated(blocks)):
         for h in range(heads):
             cols = slice((j * heads + h) * HEAD, (j * heads + h + 1) * HEAD)
             pieces_ref[n, h * group : (h + 1) * group, :] = y_ref[:, cols]
@@ -76,15 +81,13 @@
     at = lax.broadcasted_iota(jnp.int32, (chunk, HEAD), 0)
     valid = (lax.broadcasted_iota(jnp.int32, (1, positions), 1) < length).astype(jnp.float32)
     ones = jnp.ones((chunk, HEAD), jnp.bfloat16)
-    order = ordered(blocks)
+    order = rotated(blocks)
     place = [order.index(j) for j in range(blocks)]
     to = [lax.rem(z + SPLIT - behind, SPLIT) for z in range(SPLIT)]
     to = [lax.rem(z, SPLIT // 2) * 2 * lines + lax.div(z, SPLIT // 2) for z in to]
-    scales = []
-    for j in range(blocks):
-        row = squares_ref[place[j] : place[j] + 1, :group]
-        scale = lax.rsqrt(row / EMBED_DIMENSION + eps_norm)
-        scales.append(jnp.broadcast_to(scale, (HEAD, group)).T)
+    scale = lax.rsqrt(squares_ref[:, :group] / EMBED_DIMENSION + eps_norm)
+    scale = jnp.concatenate([scale, jnp.zeros((HEAD - blocks, group), jnp.float32)], axis=0).T
+    scales = [jnp.broadcast_to(scale[:, n : n + 1], (group, HEAD)) for n in place]
     product = jnp.zeros((1, 1), jnp.float32)
     squares = jnp.zeros((1, 1), jnp.float32)
     for h in range(heads):
@@ -127,13 +130,13 @@
         out_ref[j, heads * group :, :] = sums.astype(jnp.bfloat16)
 
 
-def exchanged(pieces):
+def exchanged(pieces, order):
     return lax.all_to_all(
         pieces,
         "ctx",
         split_axis=0,
         concat_axis=0,
-        axis_index_groups=[ordered(lax.axis_size("ctx"))],
+        axis_index_groups=[order(lax.axis_size("ctx"))],
         tiled=True,
     )
 
@@ -197,7 +200,7 @@
         out_specs=vmem(),
     )(y, squares)
     pieces, *turns = lax.optimization_barrier((pieces, *turns))
-    pieces = exchanged(pieces)
+    pieces = exchanged(pieces, rotated)
     squares = jnp.sum(pieces[:, heads * group : heads * group + 3, :].astype(jnp.float32), axis=1)
     behind = (lax.axis_index("pipe") == sections - 1).astype(jnp.int32)
     out = pl.pallas_call(
@@ -209,7 +212,7 @@
         out_specs=vmem(),
         compiler_params=pltpu.CompilerParams(vmem_limit_bytes=32 * 1024 * 1024),
     )(usable_extents, behind.reshape(1, 1), pieces, squares, gain, lifting, readout, *turns)
-    out = exchanged(out)
+    out = exchanged(out, ordered)
     sums = jnp.sum(out[:, heads * group, :].astype(jnp.float32), axis=0)
     route = [
         (

time: 110 us -> 110 us (level)
  blocking collectives: 40.1 us -> 43.2 us
  waiting for transfers between devices: 26.3 us -> 23.3 us
    all_to_all x1, blocking collectives: 28.6 us -> 31.6 us  [exchanged(): lax.all_to_all(pieces, 'ctx', split_axis=0, concat_axis=0, axis_index_gro...]
    all_to_all x1, waiting for transfers between devices: 19.5 us -> 16.8 us  [exchanged(): lax.all_to_all(pieces, 'ctx', split_axis=0, concat_axis=0, axis_index_gro...]
where the time goes in v7:
time: 110 us; the launch traced here: 109 us
  blocking collectives  43.2 us (39%)
  starting transfers between devices  30.3 us (28%)
  waiting for transfers between devices  23.3 us (21%)
  Pallas kernels  6.14 us (6%)
  between operations  3.83 us (3%)
  local copies, waits for them, and re-layouts  1.74 us (2%)
    all_to_all x1, blocking collectives, exchanged(): lax.all_to_all(pieces, 'ctx', split_axis=0, concat_axis=0, axis_index_gro...  31.6 us
    all_to_all x1, waiting for transfers between devices, exchanged(): lax.all_to_all(pieces, 'ctx', split_axis=0, concat_axis=0, axis_index_gro...  16.8 us
    ppermute x1, starting transfers between devices, body(): turn = lax.ppermute(turn, ('pipe', 'ctx', 'tp'), route)  15.1 us
    all_to_all x1, starting transfers between devices, exchanged(): lax.all_to_all(pieces, 'ctx', split_axis=0, concat_axis=0, axis_index_gro...  12 us
    psum x1, blocking collectives, body(): squares = lax.psum(squares, 'tp')  9.11 us
    ppermute x1, waiting for transfers between devices, body(): handed = lax.ppermute(out, ('pipe', 'ctx'), route)  5.86 us
    ppermute x1, starting transfers between devices, body(): handed = lax.ppermute(out, ('pipe', 'ctx'), route)  3.19 us
    psum x1, blocking collectives, body(): sums = lax.psum(sums, 'tp')  2.47 us
  transfers between devices with their start and end apart: 3, of which 3 were waited for; matrix products, arithmetic and copies ran while one was open for 1% of the time, Pallas kernels for 2%

profile of v7, /device:TPU:1, one launch (start us, length us, event | category | flops | bytes accessed | tf_op | source)
XLA Modules:
  0.0 109.4 jit_solution(11823105085050846433)
XLA Ops:
  0.6 1.8 %shard_map.77 = f32[1,64]{1,0:T(1,128)} custom-call(bf16[64,4096]{1,0:T(8,128)(2,1)} %bitcast.18), custom_call_target="tpu_custom_call" | custom-call | tf_op jit(solution)/shard_map/pallas_call | solution.py:167
  2.4 9.1 %psum.14.squares_ref = f32[1,64]{1,0:T(1,128)S(1)} all-reduce(f32[1,64]{1,0:T(1,128)} %shard_map.77), channel_id=1, replica_groups=mesh['pipe'=16,'ctx'=16,'tp'=2] {'tp'}, use_global_device_ids=true, to_apply=%region_0.0 | all-reduce | flops 64 | bytes 512 | tf_op jit(solution)/shard_map/psum | solution.py:173
  11.5 0.0 copy-start.3
  11.5 15.1 %collective-permute-start = (f32[1,64]{1,0:T(1,128)S(1)}, f32[1,64]{1,0:T(1,128)S(1)}, u32[]{:S(2)}, u32[]{:S(2)}) collective-permute-start(f32[1,64]{1,0:T(1,128)S(1)} %psum.14.squares_ref), channel_id=1, source_target_pairs={{1,85},{3,87},{5,81},{7,83},{9,93},{11,95},{13,89},{15,91},{17,69}... | collective-permute-start | bytes 776 | tf_op jit(solution)/shard_map/ppermute | solution.py:192
  26.7 0.0 copy-done.3
  26.7 1.9 %shard_map.78 = bf16[16,136,128]{2,1,0:T(8,128)(2,1)} custom-call(bf16[64,4096]{1,0:T(8,128)(2,1)} %bitcast.19, f32[1,64]{1,0:T(1,128)} %copy-done.3), custom_call_target="tpu_custom_call" | custom-call | tf_op jit(solution)/shard_map/pallas_call | solution.py:196
  28.6 0.0 copy-start
  28.6 0.0 copy-start.1
  28.6 0.7 collective-permute-done.refs_0_
  29.3 12.0 %all-to-all-start = ((bf16[16,136,128]{2,1,0:T(8,128)(2,1)}), bf16[16,136,128]{2,1,0:T(8,128)(2,1)S(1)}, u32[]{:S(2)}, u32[]{:S(2)}) async-start(bf16[16,136,128]{2,1,0:T(8,128)(2,1)} %shard_map.78), calls=%async_computation | async-start | bytes 1114112 | tf_op jit(solution)/shard_map/all_to_all | solution.py:134
  41.3 0.0 copy-start.2
  42.0 0.0 copy-done.2
  42.0 0.1 reduce.1
  42.1 0.7 constant_dynamic-slice_fusion
  42.8 0.0 copy-done
  42.8 0.0 copy-done.1
  42.8 16.8 %all-to-all-done.y_ref = bf16[16,136,128]{2,1,0:T(8,128)(2,1)S(1)} async-done(((bf16[16,136,128]{2,1,0:T(8,128)(2,1)}), bf16[16,136,128]{2,1,0:T(8,128)(2,1)S(1)}, u32[]{:S(2)}, u32[]{:S(2)}) %all-to-all-start) | async-done | bytes 557088 | tf_op jit(solution)/shard_map/all_to_all | solution.py:134
  59.6 2.4 %shard_map.79 = bf16[16,136,128]{2,1,0:T(8,128)(2,1)S(1)} custom-call(s32[1,1]{1,0:T(1,128)S(6)} %copy.9.length_ref, s32[1,1]{1,0:T(1,128)} %bitcast.behind_ref, bf16[16,136,128]{2,1,0:T(8,128)(2,1)S(1)} %all-to-all-done.y_ref, f32[16,128]{1,0:T(8,128)S(1)} %convert_reduce_fusion.squares_ref, bf16[2,128]{1,0:T(2,128)(2,1)S(1)} %get-tuple-element.9.gain_ref, ...), custom_call_target="tpu_custom_call" | custom-call | tf_op jit(solution)/shard_map/pallas_call | solution.py:206
  62.0 31.6 %all_to_all.10 = bf16[16,136,128]{2,1,0:T(8,128)(2,1)S(1)} all-to-all(bf16[16,136,128]{2,1,0:T(8,128)(2,1)S(1)} %shard_map.79), channel_id=1, replica_groups={{0,4,8,12,16,20,24,28,2,6,10,14,18,22,26,30},{1,5,9,13,17,21,25,29,3,7,..., dimensions={0} | all-to-all | bytes 1114112 | tf_op jit(solution)/shard_map/all_to_all | solution.py:134
  93.6 3.2 %collective-permute-start.1 = (bf16[16,136,128]{2,1,0:T(8,128)(2,1)S(1)}, bf16[16,136,128]{2,1,0:T(8,128)(2,1)S(1)}, u32[]{:S(2)}, u32[]{:S(2)}) collective-permute-start(bf16[16,136,128]{2,1,0:T(8,128)(2,1)S(1)} %all_to_all.10), channel_id=1, source_target_pairs={{0,32},{2,34},{4,36},{6,38},{8,40},{10,42},{12,44},{14,46},{16,48}... | collective-permute-start | bytes 1671176 | tf_op jit(solution)/shard_map/ppermute | solution.py:226
  96.9 2.5 %psum.15 = f32[128]{0:T(128)S(1)} all-reduce(f32[128]{0:T(128)S(1)} %fusion.1), channel_id=1, replica_groups=mesh['pipe'=16,'ctx'=16,'tp'=2] {'tp'}, use_global_device_ids=true, to_apply=%region_3.0 | all-reduce | flops 128 | bytes 1024 | tf_op jit(solution)/shard_map/psum | solution.py:232
  99.3 0.7 slice_reduce_fusion
  101.4 5.9 %collective-permute-done.1 = bf16[16,136,128]{2,1,0:T(8,128)(2,1)S(1)} collective-permute-done((bf16[16,136,128]{2,1,0:T(8,128)(2,1)S(1)}, bf16[16,136,128]{2,1,0:T(8,128)(2,1)S(1)}, u32[]{:S(2)}, u32[]{:S(2)}) %collective-permute-start.1) | collective-permute-done | bytes 557088 | tf_op jit(solution)/shard_map/ppermute | solution.py:226
  107.3 0.9 copy.8
  (4 shorter events, 0.1 us)
Async XLA Ops:
  11.5 15.2 %copy-start.3 = (f32[1,64]{1,0:T(1,128)}, f32[1,64]{1,0:T(1,128)S(1)}, u32[]{:S(2)}) copy-start(f32[1,64]{1,0:T(1,128)S(1)} %psum.14.squares_ref) | copy-start | bytes 772
  11.5 17.8 %collective-permute-start = (f32[1,64]{1,0:T(1,128)S(1)}, f32[1,64]{1,0:T(1,128)S(1)}, u32[]{:S(2)}, u32[]{:S(2)}) collective-permute-start(f32[1,64]{1,0:T(1,128)S(1)} %psum.14.squares_ref), channel_id=1, source_target_pairs={{1,85},{3,87},{5,81},{7,83},{9,93},{11,95},{13,89},{15,91},{17,69}... | collective-permute-start | bytes 776 | tf_op jit(solution)/shard_map/ppermute | solution.py:192
  28.6 14.2 %copy-start = (bf16[1,1,32,128,64]{3,4,2,1,0:T(8,128)(2,1)S(1)}, bf16[1,1,32,128,64]{3,4,2,1,0:T(8,128)(2,1)}, u32[]{:S(2)}) copy-start(bf16[1,1,32,128,64]{3,4,2,1,0:T(8,128)(2,1)} %param.8) | copy-start | bytes 1572868
  28.6 14.2 %copy-start.1 = (bf16[1,1,32,128,64]{3,4,2,1,0:T(8,128)(2,1)S(1)}, bf16[1,1,32,128,64]{3,4,2,1,0:T(8,128)(2,1)}, u32[]{:S(2)}) copy-start(bf16[1,1,32,128,64]{3,4,2,1,0:T(8,128)(2,1)} %param.9) | copy-start | bytes 1572868
  29.3 30.3 %all-to-all-start = ((bf16[16,136,128]{2,1,0:T(8,128)(2,1)}), bf16[16,136,128]{2,1,0:T(8,128)(2,1)S(1)}, u32[]{:S(2)}, u32[]{:S(2)}) async-start(bf16[16,136,128]{2,1,0:T(8,128)(2,1)} %shard_map.78), calls=%async_computation | async-start | bytes 1114112 | tf_op jit(solution)/shard_map/all_to_all | solution.py:134
  41.3 0.7 copy-start.2
  93.6 13.6 %collective-permute-start.1 = (bf16[16,136,128]{2,1,0:T(8,128)(2,1)S(1)}, bf16[16,136,128]{2,1,0:T(8,128)(2,1)S(1)}, u32[]{:S(2)}, u32[]{:S(2)}) collective-permute-start(bf16[16,136,128]{2,1,0:T(8,128)(2,1)S(1)} %all_to_all.10), channel_id=1, source_target_pairs={{0,32},{2,34},{4,36},{6,38},{8,40},{10,42},{12,44},{14,46},{16,48}... | collective-permute-start | bytes 1671176 | tf_op jit(solution)/shard_map/ppermute | solution.py:226
